TPU v7x, 128 devices: a whole 4x4x4 slice. The times are simulated.
128 devices in a mesh: seq: 16 (over x, y), head: 8 (over z, core).
Axes of the slice: x: 4, y: 4, z: 4, core: 2. Of those that a mesh axis runs over, the one named last changes fastest.
Arguments:
- query_rows: bfloat16 [16384, 2048], P('seq', 'head'), may hold values from -6 to 6
- key_rows: bfloat16 [16384, 2048], P('seq', 'head'), may hold values from -6 to 6
- value_rows: bfloat16 [16384, 2048], P('seq', 'head'), may hold values from -6 to 6
- norm_gain: float32 [2048], P('head'), may hold values from 0.5 to 1.5
- grad_out: bfloat16 [16384, 2048], P('seq', 'head'), may hold values from -6 to 6
- doc_lengths: int32 [3], replicated, may hold values from 1 to 12288, 16384 in all
- kept_blocks: int32 [16, 3, 8], replicated, may hold values from -1 to 15, as said below
Outputs:
- layer_out: bfloat16 [16384, 2048], P('seq', 'head')
- grad_queries: bfloat16 [16384, 2048], P('seq', 'head')
- grad_keys: bfloat16 [16384, 2048], P('seq', 'head')
- grad_values: bfloat16 [16384, 2048], P('seq', 'head')
- grad_gain: float32 [2048], P('head')
Inputs may be any that keep to these rules, and one draw needn't show every extreme that they name: `kept_blocks`: entry [s, l, :] lists distinct blocks of 64 positions, numbered within shard s, that shard s retains for level l, followed by -1 in the unused slots; at least half of the 8 slots are used, and for every level some shard uses all 8.
All inputs are finite; a program needn't handle non-finite values.
Results may differ from a plain program's by a relative error of at most 0.04.
Values may be sent and summed in bfloat16 or wider, within the bound.
A program may use at most 128 MiB of HBM per device.

v0:
```python
import functools

import jax
import jax.numpy as jnp
from jax import lax
from jax.experimental import pallas as pl
from jax.experimental.pallas import tpu as pltpu
from jax.sharding import PartitionSpec as P

DH = 128
TOK = 1024
SEG = 512
BLOCK = 64
KEEP = 8
LEVELS = 3
KEPT = KEEP * BLOCK
CHUNK = 256
NCH = KEPT // CHUNK
TILE = 256
WIDTH = 2048
HEADS_DEV = 2
COLS = HEADS_DEV * DH
N_SEQ = 16
N_HEAD = 8
NORM_EPS = 1e-05
SCALE = DH**-0.5
LOG2E = 1.4426950408889634
BIG = 2.0**100
LOW = -(2.0**99)
MESH = pl.DeviceIdType.MESH
F32 = jnp.float32
BF16 = jnp.bfloat16


def dot(a, b, ca, cb):
    return lax.dot_general(a, b, (((ca,), (cb,)), ((), ())), preferred_element_type=F32)


def turned(x):
    return jnp.transpose(x.astype(F32)).astype(x.dtype)


def flipped(index, bit):
    return index + bit * (1 - 2 * lax.rem(index // bit, 2))


def level_bit(level):
    return 1 + level + level // 2


def kernel(
    kept,
    lengths,
    q_ref,
    k_ref,
    v_ref,
    gain_ref,
    g_ref,
    lo_ref,
    dq_ref,
    dk_ref,
    dv_ref,
    gg_ref,
    qa,
    mk_loc,
    mk_far,
    kv_out,
    kv_in,
    gr_out,
    gr_in0,
    gr_in1,
    gr_in2,
    kt_loc,
    vt_loc,
    kt_far,
    vt_far,
    p_loc,
    p_far,
    m_run,
    m_loc,
    m_far,
    acc,
    inv_l,
    at,
    gt,
    gc,
    st,
    res,
    dot_,
    delta,
    dqt,
    dkv,
    gsum,
    inv_slot,
    kv_ss,
    kv_rs,
    gr_ss,
    gr_rs,
    st_ss,
    st_rs,
    gg_ss,
    gg_rs,
):
    me = lax.axis_index("seq")
    col = lax.axis_index("head")

    barrier = pltpu.get_barrier_semaphore()
    for bit in (1, 2, 4, 8):
        pl.semaphore_signal(barrier, inc=1, device_id=(flipped(me, bit), col), device_id_type=MESH)
    for d in range(1, N_HEAD):
        pl.semaphore_signal(
            barrier, inc=1, device_id=(me, lax.rem(col + d, N_HEAD)), device_id_type=MESH
        )

    for level in range(LEVELS):
        for slot in range(KEEP):
            block = jnp.maximum(kept[me, level, slot], 0)
            kv_out[level, slot * BLOCK : (slot + 1) * BLOCK, 0:COLS] = k_ref[block]
            kv_out[level, slot * BLOCK : (slot + 1) * BLOCK, COLS:] = v_ref[block]
    pl.semaphore_wait(barrier, 4 + N_HEAD - 1)

    def kv_copy(level, c):
        rows = pl.ds(pl.multiple_of(c * CHUNK, CHUNK), CHUNK)
        return pltpu.make_async_remote_copy(
            src_ref=kv_out.at[level, rows],
            dst_ref=kv_in.at[level, rows],
            send_sem=kv_ss.at[level, c],
            recv_sem=kv_rs.at[level, c],
            device_id=(flipped(me, level_bit(level)), col),
            device_id_type=MESH,
        )

    gr_in = (gr_in0, gr_in1, gr_in2)

    def gr_copy(level, c):
        return pltpu.make_async_remote_copy(
            src_ref=gr_out.at[level, pl.ds(c * (CHUNK // BLOCK), CHUNK // BLOCK)],
            dst_ref=gr_in[level].at[pl.ds(c * (CHUNK // BLOCK), CHUNK // BLOCK)],
            send_sem=gr_ss.at[level, c],
            recv_sem=gr_rs.at[level, c],
            device_id=(flipped(me, level_bit(level)), col),
            device_id_type=MESH,
        )

    for c in range(NCH):
        for level in (2, 0, 1):
            kv_copy(level, c).start()

    start1 = lengths[0]
    start2 = lengths[0] + lengths[1]

    def doc_of(pos):
        return (pos >= start1).astype(jnp.int32) + (pos >= start2).astype(jnp.int32)

    lane = lax.broadcasted_iota(jnp.int32, (BLOCK, DH), 1)
    row = lax.broadcasted_iota(jnp.int32, (BLOCK, DH), 0)
    for b in range(TOK // BLOCK):
        rows = slice(b * BLOCK, (b + 1) * BLOCK)
        docs = doc_of(me * TOK + b * BLOCK + row)
        same = docs == lane
        mq = jnp.where(same, 1.0, 0.0).astype(BF16)
        mk_loc[rows, :] = jnp.where(same | (lane >= 3), 0.0, -BIG).astype(BF16)
        for h in range(HEADS_DEV):
            qa[h, rows, DH:] = mq
            qa[h, rows, 0:DH] = q_ref[rows, h * DH : (h + 1) * DH]
    for level in range(LEVELS):
        partner = flipped(me, level_bit(level))
        for slot in range(KEEP):
            listed = kept[partner, level, slot]
            docs = doc_of(partner * TOK + jnp.maximum(listed, 0) * BLOCK + row)
            docs = docs - 3 * jnp.minimum(listed, 0)
            same = docs == lane
            mk_far[level, slot * BLOCK : (slot + 1) * BLOCK, :] = jnp.where(
                same | (lane >= 3), 0.0, -BIG
            ).astype(BF16)

    ones = jnp.ones((16, TOK), BF16)
    for h in range(HEADS_DEV):
        vt_loc[h, DH:, :] = ones
        for level in range(LEVELS):
            vt_far[level, h, DH:, :] = ones[:, 0:KEPT]

    for t in range(TOK // TILE):
        cols = slice(t * TILE, (t + 1) * TILE)
        blocks = slice(t * (TILE // BLOCK), (t + 1) * (TILE // BLOCK))
        kt_loc[:, cols] = turned(k_ref[blocks].reshape(TILE, COLS))
        vt = turned(v_ref[blocks].reshape(TILE, COLS))
        for h in range(HEADS_DEV):
            vt_loc[h, 0:DH, cols] = vt[h * DH : (h + 1) * DH]

    coef = SCALE * LOG2E

    @pl.loop(0, TOK // SEG)
    def _(t):
        keys = pl.ds(pl.multiple_of(t * SEG, SEG), SEG)
        blocks = pl.ds(t * (SEG // BLOCK), SEG // BLOCK)
        for h in range(HEADS_DEV):
            k = k_ref[blocks, :, h * DH : (h + 1) * DH].reshape(SEG, DH)
            ka = jnp.concatenate([k, mk_loc[keys, :]], axis=1)
            vt = vt_loc[h, :, keys]
            for j in range(SEG // TILE):
                qs = pl.ds(pl.multiple_of(t * SEG + j * TILE, TILE), TILE)
                s = dot(ka, qa[h, qs, :], 1, 1)
                m = jnp.maximum(jnp.max(s, axis=0, keepdims=True), LOW)
                p = jnp.exp2((s - m) * coef).astype(BF16)
                p_loc[h, :, qs] = p
                m_run[h, :, qs] = m
                m_loc[h, :, qs] = m
                acc[h, :, qs] = dot(vt, p, 1, 0)

    gc[...] = jnp.transpose(jnp.broadcast_to(gain_ref[...], (DH, COLS)))
    for t in range(TOK // TILE):
        cols = slice(t * TILE, (t + 1) * TILE)
        gt[:, cols] = jnp.transpose(g_ref[cols, :].astype(F32))

    @pl.loop(0, LEVELS * (TOK // BLOCK))
    def _(i):
        level = i // (TOK // BLOCK)
        b = lax.rem(i, TOK // BLOCK)
        found = jnp.int32(-1)
        for slot in range(KEEP):
            off = kept[me, level, slot] - b
            found = jnp.maximum(found, (slot + 1) * (1 - jnp.minimum(off * off, 1)) - 1)
        inv_slot[i] = found

    @pl.loop(0, LEVELS * NCH)
    def _(t):
        level = lax.rem(t + 2, 3)
        c = t // 3
        kv_copy(level, c).wait()
        rows = pl.ds(pl.multiple_of(c * CHUNK, CHUNK), CHUNK)
        kt_far[level, :, rows] = turned(kv_in[level, rows, 0:COLS])
        vt = turned(kv_in[level, rows, COLS:])
        for h in range(HEADS_DEV):
            vt_far[level, h, 0:DH, rows] = vt[h * DH : (h + 1) * DH]
        for h in range(HEADS_DEV):
            ka = jnp.concatenate(
                [kv_in[level, rows, h * DH : (h + 1) * DH], mk_far[level, rows, :]], axis=1
            )
            vta = vt_far[level, h, :, rows]
            for j in range(TOK // TILE):
                qs = slice(j * TILE, (j + 1) * TILE)
                s = dot(ka, qa[h, qs, :], 1, 1)
                m_old = m_run[h, :, qs]
                m = jnp.maximum(jnp.max(s, axis=0, keepdims=True), m_old)
                p = jnp.exp2((s - m) * coef).astype(BF16)
                p_far[level, h, rows, qs] = p
                m_run[h, :, qs] = m
                m_far[level, c, h, :, qs] = m
                acc[h, :, qs] = acc[h, :, qs] * jnp.exp2((m_old - m) * coef) + dot(vta, p, 1, 0)

    for i in range(TOK // DH):
        qs = slice(i * DH, (i + 1) * DH)
        total = jnp.zeros((1, DH), F32)
        for h in range(HEADS_DEV):
            inv = 1.0 / acc[h, DH : DH + 1, qs]
            inv_l[h, :, qs] = inv
            a = (acc[h, 0:DH, qs] * inv).astype(BF16).astype(F32)
            at[h * DH : (h + 1) * DH, qs] = a
            total = total + jnp.sum(a, axis=0, keepdims=True)
        mean = total * (1.0 / COLS)
        centred = at[:, qs] - mean
        scaled = gt[:, qs] * gc[...]
        st[0, i : i + 1, 0:128] = mean
        st[0, i : i + 1, 128:256] = jnp.sum(centred * centred, axis=0, keepdims=True)
        st[0, i : i + 1, 256:384] = jnp.sum(scaled, axis=0, keepdims=True)
        st[0, i : i + 1, 384:512] = jnp.sum(scaled * centred, axis=0, keepdims=True)

    def st_copy(d):
        return pltpu.make_async_remote_copy(
            src_ref=st.at[0],
            dst_ref=st.at[d],
            send_sem=st_ss.at[d],
            recv_sem=st_rs.at[d],
            device_id=(me, lax.rem(col + d, N_HEAD)),
            device_id_type=MESH,
        )

    for d in range(1, N_HEAD):
        st_copy(d).start()
    for d in range(1, N_HEAD):
        st_copy(d).wait()

    mean = st[0, :, 0:128]
    for d in range(1, N_HEAD):
        mean = mean + st[d, :, 0:128]
    mean = mean * (1.0 / N_HEAD)
    square = jnp.zeros((8, DH), F32)
    plain = jnp.zeros((8, DH), F32)
    cross = jnp.zeros((8, DH), F32)
    for d in range(N_HEAD):
        off = st[d, :, 0:128] - mean
        square = square + (st[d, :, 128:256] + COLS * (off * off))
        plain = plain + st[d, :, 256:384]
        cross = cross + (st[d, :, 384:512] + off * st[d, :, 256:384])
    inv_std = lax.rsqrt(square * (1.0 / WIDTH) + NORM_EPS)
    res[:, 0:128] = mean
    res[:, 128:256] = inv_std
    res[:, 256:384] = plain * (1.0 / WIDTH)
    res[:, 384:512] = inv_std * cross * (1.0 / WIDTH)

    for i in range(TOK // DH):
        qs = slice(i * DH, (i + 1) * DH)
        inv_std = res[i : i + 1, 128:256]
        normed = (at[:, qs] - res[i : i + 1, 0:128]) * inv_std
        scaled = gt[:, qs] * gc[...]
        do = inv_std * (scaled - res[i : i + 1, 256:384] - normed * res[i : i + 1, 384:512])
        do = do.astype(BF16)
        dot_[:, qs] = do
        both = do.astype(F32) * at[:, qs]
        for h in range(HEADS_DEV):
            delta[h, :, qs] = jnp.sum(both[h * DH : (h + 1) * DH], axis=0, keepdims=True)

    def back(h, qs, m, v, kt, p):
        factor = jnp.exp2((m - m_run[h, :, qs]) * coef) * inv_l[h, :, qs]
        do = (dot_[h * DH : (h + 1) * DH, qs].astype(F32) * factor).astype(BF16)
        dp = dot(v, do, 1, 0)
        ds = (p.astype(F32) * (dp - factor * delta[h, :, qs])).astype(BF16)
        dq = dot(kt, ds, 1, 0)
        dk = dot(ds, qa[h, qs, 0:DH], 1, 0)
        dv = dot(p, do, 1, 1)
        return dq, dk, dv

    dqt[...] = jnp.zeros_like(dqt)

    @pl.loop(0, LEVELS * NCH)
    def _(t):
        level = lax.rem(4 - lax.rem(t, 3), 3)
        c = t // 3
        rows = pl.ds(pl.multiple_of(c * CHUNK, CHUNK), CHUNK)
        for h in range(HEADS_DEV):
            hs = slice(h * DH, (h + 1) * DH)
            v = kv_in[level, rows, COLS + h * DH : COLS + (h + 1) * DH]
            kt = kt_far[level, hs, rows]
            dk_sum = jnp.zeros((CHUNK, DH), F32)
            dv_sum = jnp.zeros((CHUNK, DH), F32)
            for j in range(TOK // TILE):
                qs = slice(j * TILE, (j + 1) * TILE)
                dq, dk, dv = back(h, qs, m_far[level, c, h, :, qs], v, kt, p_far[level, h, rows, qs])
                dqt[hs, qs] += dq
                dk_sum = dk_sum + dk
                dv_sum = dv_sum + dv
            blocks = pl.ds(c * (CHUNK // BLOCK), CHUNK // BLOCK)
            vs = slice(COLS + h * DH, COLS + (h + 1) * DH)
            shape = (CHUNK // BLOCK, BLOCK, DH)
            gr_out[level, blocks, :, hs] = (dk_sum * SCALE).astype(BF16).reshape(shape)
            gr_out[level, blocks, :, vs] = dv_sum.astype(BF16).reshape(shape)
        for one in range(LEVELS):
            pl.when(level == one)(lambda one=one: gr_copy(one, c).start())

    gain_part = jnp.zeros((COLS, DH), F32)
    for i in range(TOK // DH):
        qs = slice(i * DH, (i + 1) * DH)
        normed = (at[:, qs] - res[i : i + 1, 0:128]) * res[i : i + 1, 128:256]
        gain_part = gain_part + gt[:, qs] * normed
        lo_ref[qs, :] = jnp.transpose(normed * gc[...]).astype(BF16)
    gsum[0] = jnp.broadcast_to(
        jnp.sum(jnp.transpose(gain_part), axis=0, keepdims=True), (8, COLS)
    )

    def gg_copy(stage):
        return pltpu.make_async_remote_copy(
            src_ref=gsum.at[2 * stage],
            dst_ref=gsum.at[2 * stage + 1],
            send_sem=gg_ss.at[stage],
            recv_sem=gg_rs.at[stage],
            device_id=(flipped(me, 1 << stage), col),
            device_id_type=MESH,
        )

    gg_copy(0).start()

    @pl.loop(0, TOK // SEG)
    def _(t):
        keys = pl.ds(pl.multiple_of(t * SEG, SEG), SEG)
        blocks = pl.ds(t * (SEG // BLOCK), SEG // BLOCK)
        for h in range(HEADS_DEV):
            hs = slice(h * DH, (h + 1) * DH)
            v = v_ref[blocks, :, hs].reshape(SEG, DH)
            kt = kt_loc[hs, keys]
            dk_sum = jnp.zeros((SEG, DH), F32)
            dv_sum = jnp.zeros((SEG, DH), F32)
            for j in range(SEG // TILE):
                qs = pl.ds(pl.multiple_of(t * SEG + j * TILE, TILE), TILE)
                dq, dk, dv = back(h, qs, m_loc[h, :, qs], v, kt, p_loc[h, :, qs])
                dqt[hs, qs] += dq
                dk_sum = dk_sum + dk
                dv_sum = dv_sum + dv
            dkv[keys, hs] = dk_sum * SCALE
            dkv[keys, COLS + h * DH : COLS + (h + 1) * DH] = dv_sum

    for stage in range(4):
        gg_copy(stage).wait()
        gsum[2 * stage + 2] = gsum[2 * stage] + gsum[2 * stage + 1]
        if stage < 3:
            gg_copy(stage + 1).start()
        for t in range(stage, TOK // TILE, 4):
            cols = slice(t * TILE, (t + 1) * TILE)
            dq_ref[cols, :] = jnp.transpose(dqt[:, cols] * SCALE).astype(BF16)
    gg_ref[...] = gsum[8, 0:1, :]

    for level in (2, 0, 1):
        for c in range(NCH):
            gr_copy(level, c).wait()

        @pl.loop(0, TOK // BLOCK)
        def _(b):
            slot = inv_slot[level * (TOK // BLOCK) + b]
            rows = pl.ds(pl.multiple_of(b * BLOCK, BLOCK), BLOCK)
            part = gr_in[level][jnp.maximum(slot, 0)].astype(F32)
            total = dkv[rows, :] + part * jnp.minimum(slot + 1, 1).astype(F32)
            if level == 1:
                dk_ref[rows, :] = total[:, 0:COLS].astype(BF16)
                dv_ref[rows, :] = total[:, COLS:].astype(BF16)
            else:
                dkv[rows, :] = total


def local(query_rows, key_rows, value_rows, norm_gain, grad_out, doc_lengths, kept_blocks):
    vmem = pl.BlockSpec(memory_space=pltpu.VMEM)
    smem = pl.BlockSpec(memory_space=pltpu.SMEM)
    rows = jax.ShapeDtypeStruct((TOK, COLS), BF16)
    dma = pltpu.SemaphoreType.DMA
    scratch = [
        pltpu.VMEM((HEADS_DEV, TOK, 2 * DH), BF16),
        pltpu.VMEM((TOK, DH), BF16),
        pltpu.VMEM((LEVELS, KEPT, DH), BF16),
        pltpu.VMEM((LEVELS, KEPT, 2 * COLS), BF16),
        pltpu.VMEM((LEVELS, KEPT, 2 * COLS), BF16),
        pltpu.VMEM((LEVELS, KEEP, BLOCK, 2 * COLS), BF16),
        pltpu.VMEM((KEEP, BLOCK, 2 * COLS), BF16),
        pltpu.VMEM((KEEP, BLOCK, 2 * COLS), BF16),
        pltpu.VMEM((KEEP, BLOCK, 2 * COLS), BF16),
        pltpu.VMEM((COLS, TOK), BF16),
        pltpu.VMEM((HEADS_DEV, DH + 16, TOK), BF16),
        pltpu.VMEM((LEVELS, COLS, KEPT), BF16),
        pltpu.VMEM((LEVELS, HEADS_DEV, DH + 16, KEPT), BF16),
        pltpu.VMEM((HEADS_DEV, SEG, TOK), BF16),
        pltpu.VMEM((LEVELS, HEADS_DEV, KEPT, TOK), BF16),
        pltpu.VMEM((HEADS_DEV, 1, TOK), F32),
        pltpu.VMEM((HEADS_DEV, 1, TOK), F32),
        pltpu.VMEM((LEVELS, NCH, HEADS_DEV, 1, TOK), F32),
        pltpu.VMEM((HEADS_DEV, DH + 16, TOK), F32),
        pltpu.VMEM((HEADS_DEV, 1, TOK), F32),
        pltpu.VMEM((COLS, TOK), F32),
        pltpu.VMEM((COLS, TOK), F32),
        pltpu.VMEM((COLS, DH), F32),
        pltpu.VMEM((N_HEAD, 8, 512), F32),
        pltpu.VMEM((8, 512), F32),
        pltpu.VMEM((COLS, TOK), BF16),
        pltpu.VMEM((HEADS_DEV, 1, TOK), F32),
        pltpu.VMEM((COLS, TOK), F32),
        pltpu.VMEM((TOK, 2 * COLS), F32),
        pltpu.VMEM((9, 8, COLS), F32),
        pltpu.SMEM((LEVELS * (TOK // BLOCK),), jnp.int32),
        dma((LEVELS, NCH)),
        dma((LEVELS, NCH)),
        dma((LEVELS, NCH)),
        dma((LEVELS, NCH)),
        dma((N_HEAD,)),
        dma((N_HEAD,)),
        dma((4,)),
        dma((4,)),
    ]
    out = pl.pallas_call(
        kernel,
        out_shape=[rows, rows, rows, rows, jax.ShapeDtypeStruct((1, COLS), F32)],
        in_specs=[smem, smem, vmem, vmem, vmem, vmem, vmem],
        out_specs=[vmem] * 5,
        scratch_shapes=scratch,
        compiler_params=pltpu.CompilerParams(
            collective_id=0, has_side_effects=True, vmem_limit_bytes=56 * 1024 * 1024
        ),
        name="attention",
    )(
        kept_blocks,
        doc_lengths,
        query_rows,
        key_rows.reshape(TOK // BLOCK, BLOCK, COLS),
        value_rows.reshape(TOK // BLOCK, BLOCK, COLS),
        norm_gain.reshape(1, COLS),
        grad_out,
    )
    return out[0], out[1], out[2], out[3], out[4].reshape(COLS)


def solution(mesh):
    rows = P("seq", "head")
    in_specs = (rows, rows, rows, P("head"), rows, P(), P())
    out_specs = (rows, rows, rows, rows, P("head"))
    return jax.shard_map(local, mesh=mesh, in_specs=in_specs, out_specs=out_specs, check_vma=False)
```

profile of v0, /device:TPU:0, one launch (start us, length us, event | category | flops | bytes accessed | tf_op | source)
XLA Modules:
  0.0 86.8 jit_solution(7645037327659869307)
XLA Ops:
  0.6 1.4 %copy.12.kept = s32[16,3,8]{2,1,0:T(4,128)} copy(s32[16,3,8]{0,2,1:T(8,128)} %param.13) | data formatting | bytes 3072 | tf_op args[6]
  2.0 79.0 %attention.1 = (bf16[1024,256]{1,0:T(8,128)(2,1)}, bf16[1024,256]{1,0:T(8,128)(2,1)}, bf16[1024,256]{1,0:T(8,128)(2,1)}, bf16[1024,256]{1,0:T(8,128)(2,1)}, f32[1,256]{1,0:T(1,128)}) custom-call(s32[16,3,8]{2,1,0:T(4,128)} %copy.12.kept, s32[3]{0:T(128)} %lengths.1, bf16[1024,256]{1,0:T(8,128)(2,1)} %q_ref.1, bf16[16,64,256]{2,1,0:T(8,128)(2,1)} %bitcast.4, ...), custom_call_target="tpu_custom_call" | custom-call | tf_op jit(solution)/shard_map/attention/pallas_call | solution.py:465
  81.1 0.0 copy-start.2
  81.1 1.9 %copy.18 = bf16[1024,256]{1,0:T(8,128)(2,1)} copy(bf16[1024,256]{1,0:T(8,128)(2,1)} %get-tuple-element.20) | data formatting | bytes 1048576
  83.0 0.0 copy-done.2
  83.0 0.0 copy-start.1
  83.0 0.8 copy.19
  83.8 0.4 copy-done.1
  84.2 0.0 copy-start
  84.2 0.8 copy.20
  85.0 0.4 copy-done
  85.5 0.0 copy-start.3
  85.5 0.8 copy.21
  86.3 0.0 copy-done.3
  86.3 0.6 copy.22
Async XLA Ops:
  81.1 1.9 %copy-start.2 = (bf16[1024,256]{1,0:T(8,128)(2,1)S(1)}, bf16[1024,256]{1,0:T(8,128)(2,1)}, u32[]{:S(2)}) copy-start(bf16[1024,256]{1,0:T(8,128)(2,1)} %get-tuple-element.21) | copy-start | bytes 1572868
  83.0 1.2 %copy-start.1 = (bf16[1024,256]{1,0:T(8,128)(2,1)S(1)}, bf16[1024,256]{1,0:T(8,128)(2,1)}, u32[]{:S(2)}) copy-start(bf16[1024,256]{1,0:T(8,128)(2,1)} %get-tuple-element.22) | copy-start | bytes 1572868
  84.2 1.2 %copy-start = (bf16[1024,256]{1,0:T(8,128)(2,1)S(1)}, bf16[1024,256]{1,0:T(8,128)(2,1)}, u32[]{:S(2)}) copy-start(bf16[1024,256]{1,0:T(8,128)(2,1)} %get-tuple-element.23) | copy-start | bytes 1572868
  85.5 0.8 copy-start.3
where the time goes:
time: 87.2 us; the launch traced here: 86.8 us
  Pallas kernels  79 us (91%)
  local copies, waits for them, and re-layouts  7.15 us (8%)
    pallas_call x1, Pallas kernels, local(): pl.pallas_call(kernel, out_shape=[rows, rows, rows, rows, jax.ShapeDtypeS...  79 us
    unnamed x14, local copies, waits for them, and re-layouts  7.15 us

commit v1 on v0

--- a/solution.py
+++ b/solution.py
@@ -51,6 +51,16 @@
 def kernel(
     kept,
     lengths,
+    q_hbm,
+    k_hbm,
+    v_hbm,
+    gain_hbm,
+    g_hbm,
+    lo_hbm,
+    dq_hbm,
+    part_hbm,
+    gr_hbm,
+    gg_ref,
     q_ref,
     k_ref,
     v_ref,
@@ -58,17 +68,12 @@
     g_ref,
     lo_ref,
     dq_ref,
-    dk_ref,
-    dv_ref,
-    gg_ref,
     qa,
     mk_loc,
     mk_far,
     kv_out,
     kv_in,
     gr_out,
-    gr_in0,
-    gr_in1,
     gr_in2,
     kt_loc,
     vt_loc,
@@ -100,6 +105,7 @@
     st_rs,
     gg_ss,
     gg_rs,
+    io,
 ):
     me = lax.axis_index("seq")
     col = lax.axis_index("head")
@@ -112,9 +118,26 @@
             barrier, inc=1, device_id=(me, lax.rem(col + d, N_HEAD)), device_id_type=MESH
         )
 
+    loads = [
+        pltpu.make_async_copy(src, dst, io.at[i])
+        for i, (src, dst) in enumerate(
+            (
+                (k_hbm, k_ref),
+                (v_hbm, v_ref),
+                (q_hbm, q_ref),
+                (g_hbm, g_ref),
+                (gain_hbm, gain_ref),
+            )
+        )
+    ]
+    for load in loads:
+        load.start()
+    loads[0].wait()
+    loads[1].wait()
+
     for level in range(LEVELS):
         for slot in range(KEEP):
-            block = jnp.maximum(kept[me, level, slot], 0)
+            block = jnp.maximum(kept[level, slot, me], 0)
             kv_out[level, slot * BLOCK : (slot + 1) * BLOCK, 0:COLS] = k_ref[block]
             kv_out[level, slot * BLOCK : (slot + 1) * BLOCK, COLS:] = v_ref[block]
     pl.semaphore_wait(barrier, 4 + N_HEAD - 1)
@@ -130,14 +153,14 @@
             device_id_type=MESH,
         )
 
-    gr_in = (gr_in0, gr_in1, gr_in2)
-
-    def gr_copy(level, c):
+    def gr_copy(level, c, h):
+        blocks = pl.ds(c * (CHUNK // BLOCK), CHUNK // BLOCK)
+        dst = gr_in2 if level == 2 else gr_hbm.at[level]
         return pltpu.make_async_remote_copy(
-            src_ref=gr_out.at[level, pl.ds(c * (CHUNK // BLOCK), CHUNK // BLOCK)],
-            dst_ref=gr_in[level].at[pl.ds(c * (CHUNK // BLOCK), CHUNK // BLOCK)],
-            send_sem=gr_ss.at[level, c],
-            recv_sem=gr_rs.at[level, c],
+            src_ref=gr_out.at[level, h, blocks],
+            dst_ref=dst.at[h, blocks],
+            send_sem=gr_ss.at[level, c, h],
+            recv_sem=gr_rs.at[level, c, h],
             device_id=(flipped(me, level_bit(level)), col),
             device_id_type=MESH,
         )
@@ -146,6 +169,8 @@
         for level in (2, 0, 1):
             kv_copy(level, c).start()
 
+    for load in loads[2:]:
+        load.wait()
     start1 = lengths[0]
     start2 = lengths[0] + lengths[1]
 
@@ -166,7 +191,7 @@
     for level in range(LEVELS):
         partner = flipped(me, level_bit(level))
         for slot in range(KEEP):
-            listed = kept[partner, level, slot]
+            listed = kept[level, slot, partner]
             docs = doc_of(partner * TOK + jnp.maximum(listed, 0) * BLOCK + row)
             docs = docs - 3 * jnp.minimum(listed, 0)
             same = docs == lane
@@ -213,15 +238,13 @@
         cols = slice(t * TILE, (t + 1) * TILE)
         gt[:, cols] = jnp.transpose(g_ref[cols, :].astype(F32))
 
-    @pl.loop(0, LEVELS * (TOK // BLOCK))
-    def _(i):
-        level = i // (TOK // BLOCK)
-        b = lax.rem(i, TOK // BLOCK)
+    @pl.loop(0, TOK // BLOCK)
+    def _(b):
         found = jnp.int32(-1)
         for slot in range(KEEP):
-            off = kept[me, level, slot] - b
+            off = kept[2, slot, me] - b
             found = jnp.maximum(found, (slot + 1) * (1 - jnp.minimum(off * off, 1)) - 1)
-        inv_slot[i] = found
+        inv_slot[b] = found
 
     @pl.loop(0, LEVELS * NCH)
     def _(t):
@@ -299,6 +322,7 @@
     res[:, 256:384] = plain * (1.0 / WIDTH)
     res[:, 384:512] = inv_std * cross * (1.0 / WIDTH)
 
+    gain_part = jnp.zeros((COLS, DH), F32)
     for i in range(TOK // DH):
         qs = slice(i * DH, (i + 1) * DH)
         inv_std = res[i : i + 1, 128:256]
@@ -307,6 +331,7 @@
         do = inv_std * (scaled - res[i : i + 1, 256:384] - normed * res[i : i + 1, 384:512])
         do = do.astype(BF16)
         dot_[:, qs] = do
+        gain_part = gain_part + gt[:, qs] * normed
         both = do.astype(F32) * at[:, qs]
         for h in range(HEADS_DEV):
             delta[h, :, qs] = jnp.sum(both[h * DH : (h + 1) * DH], axis=0, keepdims=True)
@@ -323,9 +348,29 @@
 
     dqt[...] = jnp.zeros_like(dqt)
 
+    gsum[0] = jnp.broadcast_to(jnp.sum(jnp.transpose(gain_part), axis=0, keepdims=True), (8, COLS))
+
+    def gg_copy(stage):
+        return pltpu.make_async_remote_copy(
+            src_ref=gsum.at[2 * stage],
+            dst_ref=gsum.at[2 * stage + 1],
+            send_sem=gg_ss.at[stage],
+            recv_sem=gg_rs.at[stage],
+            device_id=(flipped(me, 1 << stage), col),
+            device_id_type=MESH,
+        )
+
+    def gg_end(stage):
+        gg_copy(stage).wait()
+        gsum[2 * stage + 2] = gsum[2 * stage] + gsum[2 * stage + 1]
+        if stage < 3:
+            gg_copy(stage + 1).start()
+
+    gg_copy(0).start()
+
     @pl.loop(0, LEVELS * NCH)
     def _(t):
-        level = lax.rem(4 - lax.rem(t, 3), 3)
+        level = lax.rem(t, 3)
         c = t // 3
         rows = pl.ds(pl.multiple_of(c * CHUNK, CHUNK), CHUNK)
         for h in range(HEADS_DEV):
@@ -341,34 +386,23 @@
                 dk_sum = dk_sum + dk
                 dv_sum = dv_sum + dv
             blocks = pl.ds(c * (CHUNK // BLOCK), CHUNK // BLOCK)
-            vs = slice(COLS + h * DH, COLS + (h + 1) * DH)
             shape = (CHUNK // BLOCK, BLOCK, DH)
-            gr_out[level, blocks, :, hs] = (dk_sum * SCALE).astype(BF16).reshape(shape)
-            gr_out[level, blocks, :, vs] = dv_sum.astype(BF16).reshape(shape)
-        for one in range(LEVELS):
-            pl.when(level == one)(lambda one=one: gr_copy(one, c).start())
-
-    gain_part = jnp.zeros((COLS, DH), F32)
+            gr_out[level, h, blocks, :, 0:DH] = (dk_sum * SCALE).astype(BF16).reshape(shape)
+            gr_out[level, h, blocks, :, DH:] = dv_sum.astype(BF16).reshape(shape)
+            if h == 0:
+                pl.when(t == 0)(lambda: gg_end(0))
+                pl.when(t == 1)(lambda: gg_end(2))
+            else:
+                pl.when(t == 0)(lambda: gg_end(1))
+            for one in range(LEVELS):
+                pl.when(level == one)(lambda one=one, h=h: gr_copy(one, c, h).start())
+
     for i in range(TOK // DH):
         qs = slice(i * DH, (i + 1) * DH)
         normed = (at[:, qs] - res[i : i + 1, 0:128]) * res[i : i + 1, 128:256]
-        gain_part = gain_part + gt[:, qs] * normed
         lo_ref[qs, :] = jnp.transpose(normed * gc[...]).astype(BF16)
-    gsum[0] = jnp.broadcast_to(
-        jnp.sum(jnp.transpose(gain_part), axis=0, keepdims=True), (8, COLS)
-    )
-
-    def gg_copy(stage):
-        return pltpu.make_async_remote_copy(
-            src_ref=gsum.at[2 * stage],
-            dst_ref=gsum.at[2 * stage + 1],
-            send_sem=gg_ss.at[stage],
-            recv_sem=gg_rs.at[stage],
-            device_id=(flipped(me, 1 << stage), col),
-            device_id_type=MESH,
-        )
-
-    gg_copy(0).start()
+    lo_copy = pltpu.make_async_copy(lo_ref, lo_hbm, io.at[0])
+    lo_copy.start()
 
     @pl.loop(0, TOK // SEG)
     def _(t):
@@ -389,48 +423,88 @@
             dkv[keys, hs] = dk_sum * SCALE
             dkv[keys, COLS + h * DH : COLS + (h + 1) * DH] = dv_sum
 
-    for stage in range(4):
-        gg_copy(stage).wait()
-        gsum[2 * stage + 2] = gsum[2 * stage] + gsum[2 * stage + 1]
-        if stage < 3:
-            gg_copy(stage + 1).start()
-        for t in range(stage, TOK // TILE, 4):
-            cols = slice(t * TILE, (t + 1) * TILE)
-            dq_ref[cols, :] = jnp.transpose(dqt[:, cols] * SCALE).astype(BF16)
+    for t in range(TOK // TILE):
+        cols = slice(t * TILE, (t + 1) * TILE)
+        dq_ref[cols, :] = jnp.transpose(dqt[:, cols] * SCALE).astype(BF16)
+    dq_copy = pltpu.make_async_copy(dq_ref, dq_hbm, io.at[1])
+    dq_copy.start()
+    gg_end(3)
     gg_ref[...] = gsum[8, 0:1, :]
 
-    for level in (2, 0, 1):
-        for c in range(NCH):
-            gr_copy(level, c).wait()
-
-        @pl.loop(0, TOK // BLOCK)
-        def _(b):
-            slot = inv_slot[level * (TOK // BLOCK) + b]
-            rows = pl.ds(pl.multiple_of(b * BLOCK, BLOCK), BLOCK)
-            part = gr_in[level][jnp.maximum(slot, 0)].astype(F32)
-            total = dkv[rows, :] + part * jnp.minimum(slot + 1, 1).astype(F32)
-            if level == 1:
-                dk_ref[rows, :] = total[:, 0:COLS].astype(BF16)
-                dv_ref[rows, :] = total[:, COLS:].astype(BF16)
-            else:
-                dkv[rows, :] = total
+    for c in range(NCH):
+        for h in range(HEADS_DEV):
+            gr_copy(2, c, h).wait()
+
+    @pl.loop(0, TOK // BLOCK)
+    def _(b):
+        slot = inv_slot[b]
+        rows = pl.ds(pl.multiple_of(b * BLOCK, BLOCK), BLOCK)
+        used = jnp.minimum(slot + 1, 1).astype(F32)
+        for h in range(HEADS_DEV):
+            part = gr_in2[h, jnp.maximum(slot, 0)].astype(F32) * used
+            dkv[rows, h * DH : (h + 1) * DH] += part[:, 0:DH]
+            dkv[rows, COLS + h * DH : COLS + (h + 1) * DH] += part[:, DH:]
+
+    part_copy = pltpu.make_async_copy(dkv, part_hbm, io.at[2])
+    part_copy.start()
+    for c in range(NCH):
+        for level in range(2):
+            for h in range(HEADS_DEV):
+                gr_copy(level, c, h).wait()
+    lo_copy.wait()
+    dq_copy.wait()
+    part_copy.wait()
+
+
+def finish(
+    kept, lo_in, dq_in, part_in, gr_in, gg_in, lo_ref, dq_ref, dk_ref, dv_ref, gg_ref
+):
+    me = lax.axis_index("seq")
+    step = pl.program_id(0)
+    lo_ref[...] = lo_in[...]
+    dq_ref[...] = dq_in[...]
+    gg_ref[...] = gg_in[...]
+    for i in range(TILE // BLOCK):
+        rows = slice(i * BLOCK, (i + 1) * BLOCK)
+        block = step * (TILE // BLOCK) + i
+        total = part_in[rows, :]
+        dk = [total[:, h * DH : (h + 1) * DH] for h in range(HEADS_DEV)]
+        dv = [total[:, COLS + h * DH : COLS + (h + 1) * DH] for h in range(HEADS_DEV)]
+        for level in range(2):
+            found = jnp.int32(-1)
+            for slot in range(KEEP):
+                found = jnp.where(kept[level, slot, me] == block, jnp.int32(slot), found)
+            used = jnp.minimum(found + 1, 1).astype(F32)
+            for h in range(HEADS_DEV):
+                part = gr_in[level, h, jnp.maximum(found, 0)].astype(F32) * used
+                dk[h] = dk[h] + part[:, 0:DH]
+                dv[h] = dv[h] + part[:, DH:]
+        for h in range(HEADS_DEV):
+            dk_ref[rows, h * DH : (h + 1) * DH] = dk[h].astype(BF16)
+            dv_ref[rows, h * DH : (h + 1) * DH] = dv[h].astype(BF16)
 
 
 def local(query_rows, key_rows, value_rows, norm_gain, grad_out, doc_lengths, kept_blocks):
     vmem = pl.BlockSpec(memory_space=pltpu.VMEM)
     smem = pl.BlockSpec(memory_space=pltpu.SMEM)
+    hbm = pl.BlockSpec(memory_space=pl.ANY)
     rows = jax.ShapeDtypeStruct((TOK, COLS), BF16)
     dma = pltpu.SemaphoreType.DMA
     scratch = [
+        pltpu.VMEM((TOK, COLS), BF16),
+        pltpu.VMEM((TOK // BLOCK, BLOCK, COLS), BF16),
+        pltpu.VMEM((TOK // BLOCK, BLOCK, COLS), BF16),
+        pltpu.VMEM((1, COLS), F32),
+        pltpu.VMEM((TOK, COLS), BF16),
+        pltpu.VMEM((TOK, COLS), BF16),
+        pltpu.VMEM((TOK, COLS), BF16),
         pltpu.VMEM((HEADS_DEV, TOK, 2 * DH), BF16),
         pltpu.VMEM((TOK, DH), BF16),
         pltpu.VMEM((LEVELS, KEPT, DH), BF16),
         pltpu.VMEM((LEVELS, KEPT, 2 * COLS), BF16),
         pltpu.VMEM((LEVELS, KEPT, 2 * COLS), BF16),
-        pltpu.VMEM((LEVELS, KEEP, BLOCK, 2 * COLS), BF16),
-        pltpu.VMEM((KEEP, BLOCK, 2 * COLS), BF16),
-        pltpu.VMEM((KEEP, BLOCK, 2 * COLS), BF16),
-        pltpu.VMEM((KEEP, BLOCK, 2 * COLS), BF16),
+        pltpu.VMEM((LEVELS, HEADS_DEV, KEEP, BLOCK, 2 * DH), BF16),
+        pltpu.VMEM((HEADS_DEV, KEEP, BLOCK, 2 * DH), BF16),
         pltpu.VMEM((COLS, TOK), BF16),
         pltpu.VMEM((HEADS_DEV, DH + 16, TOK), BF16),
         pltpu.VMEM((LEVELS, COLS, KEPT), BF16),
@@ -452,28 +526,37 @@
         pltpu.VMEM((COLS, TOK), F32),
         pltpu.VMEM((TOK, 2 * COLS), F32),
         pltpu.VMEM((9, 8, COLS), F32),
-        pltpu.SMEM((LEVELS * (TOK // BLOCK),), jnp.int32),
+        pltpu.SMEM((TOK // BLOCK,), jnp.int32),
         dma((LEVELS, NCH)),
         dma((LEVELS, NCH)),
-        dma((LEVELS, NCH)),
-        dma((LEVELS, NCH)),
+        dma((LEVELS, NCH, HEADS_DEV)),
+        dma((LEVELS, NCH, HEADS_DEV)),
         dma((N_HEAD,)),
         dma((N_HEAD,)),
         dma((4,)),
         dma((4,)),
+        dma((5,)),
     ]
-    out = pl.pallas_call(
+    kept = jnp.transpose(kept_blocks, (1, 2, 0))
+    gain_row = jax.ShapeDtypeStruct((1, COLS), F32)
+    lo, dq, part, returned, gain = pl.pallas_call(
         kernel,
-        out_shape=[rows, rows, rows, rows, jax.ShapeDtypeStruct((1, COLS), F32)],
-        in_specs=[smem, smem, vmem, vmem, vmem, vmem, vmem],
-        out_specs=[vmem] * 5,
+        out_shape=[
+            rows,
+            rows,
+            jax.ShapeDtypeStruct((TOK, 2 * COLS), F32),
+            jax.ShapeDtypeStruct((2, HEADS_DEV, KEEP, BLOCK, 2 * DH), BF16),
+            gain_row,
+        ],
+        in_specs=[smem, smem] + [hbm] * 5,
+        out_specs=[hbm] * 4 + [vmem],
         scratch_shapes=scratch,
         compiler_params=pltpu.CompilerParams(
             collective_id=0, has_side_effects=True, vmem_limit_bytes=56 * 1024 * 1024
         ),
         name="attention",
     )(
-        kept_blocks,
+        kept,
         doc_lengths,
         query_rows,
         key_rows.reshape(TOK // BLOCK, BLOCK, COLS),
@@ -481,7 +564,25 @@
         norm_gain.reshape(1, COLS),
         grad_out,
     )
-    return out[0], out[1], out[2], out[3], out[4].reshape(COLS)
+    tile = pl.BlockSpec((TILE, COLS), lambda i: (i, 0))
+    gain_spec = pl.BlockSpec((1, COLS), lambda i: (0, 0))
+    lo, dq, dk, dv, gain = pl.pallas_call(
+        finish,
+        grid=(TOK // TILE,),
+        out_shape=[rows, rows, rows, rows, gain_row],
+        in_specs=[
+            smem,
+            tile,
+            tile,
+            pl.BlockSpec((TILE, 2 * COLS), lambda i: (i, 0)),
+            pl.BlockSpec(returned.shape, lambda i: (0, 0, 0, 0, 0)),
+            gain_spec,
+        ],
+        out_specs=[tile, tile, tile, tile, gain_spec],
+        compiler_params=pltpu.CompilerParams(vmem_limit_bytes=60 * 1024 * 1024),
+        name="finish",
+    )(kept, lo, dq, part, returned, gain)
+    return lo, dq, dk, dv, gain.reshape(COLS)
 
 
 def solution(mesh):

time: 87.2 us -> 72.7 us (0.83)
  Pallas kernels: 79 us -> 71.8 us
  local copies, waits for them, and re-layouts: 7.15 us -> 0 us
    pallas_call x1 -> x2, Pallas kernels: 79 us -> 71.8 us  [the longest x1 67.2 us: local(): pl.pallas_call(kernel, out_shape=[rows, rows, jax.ShapeDtypeStruct((TOK,...]
    unnamed x14 -> x0, local copies, waits for them, and re-layouts: 7.15 us -> none
where the time goes in v1:
time: 72.7 us; the launch traced here: 72.4 us
  Pallas kernels  71.8 us (99%)
    pallas_call x1, Pallas kernels, local(): pl.pallas_call(kernel, out_shape=[rows, rows, jax.ShapeDtypeStruct((TOK,...  67.2 us
    pallas_call x1, Pallas kernels, local(): pl.pallas_call(finish, grid=(TOK // TILE,), out_shape=[rows, rows, rows,...  4.62 us

profile of v1, /device:TPU:0, one launch (start us, length us, event | category | flops | bytes accessed | tf_op | source)
XLA Modules:
  0.0 72.4 jit_solution(5227395762826374800)
XLA Ops:
  0.6 67.2 %attention.1 = (bf16[1024,256]{1,0:T(8,128)(2,1)}, bf16[1024,256]{1,0:T(8,128)(2,1)}, f32[1024,512]{1,0:T(8,128)}, bf16[2,2,8,64,256]{4,3,2,1,0:T(8,128)(2,1)}, f32[1,256]{1,0:T(1,128)}) custom-call(s32[3,8,16]{2,1,0:T(8,128)} %bitcast.7, s32[3]{0:T(128)} %lengths.1, bf16[1024,256]{1,0:T(8,128)(2,1)} %q_hbm.1, bf16[16,64,256]{2,1,0:T(8,128)(2,1)} %bitcast.5, ...), custom_call_target="tpu_custom_call" | custom-call | tf_op jit(solution)/shard_map/attention/pallas_call | solution.py:542
  67.8 4.6 %finish.1 = (bf16[1024,256]{1,0:T(8,128)(2,1)}, bf16[1024,256]{1,0:T(8,128)(2,1)}, bf16[1024,256]{1,0:T(8,128)(2,1)}, bf16[1024,256]{1,0:T(8,128)(2,1)}, f32[1,256]{1,0:T(1,128)}) custom-call(s32[3,8,16]{2,1,0:T(8,128)} %bitcast.8, bf16[1024,256]{1,0:T(8,128)(2,1)} %get-tuple-element.15.lo_in, bf16[1024,256]{1,0:T(8,128)(2,1)} %get-tuple-element.16.dq_in, ...), custom_call_target="tpu_custom_call" | custom-call | tf_op jit(solution)/shard_map/finish/pallas_call | solution.py:569

commit v2 on v1

--- a/solution.py
+++ b/solution.py
@@ -49,7 +49,7 @@
 
 
 def kernel(
-    kept,
+    kept_hbm,
     lengths,
     q_hbm,
     k_hbm,
@@ -61,6 +61,7 @@
     part_hbm,
     gr_hbm,
     gg_ref,
+    kept,
     q_ref,
     k_ref,
     v_ref,
@@ -124,6 +125,7 @@
             (
                 (k_hbm, k_ref),
                 (v_hbm, v_ref),
+                (kept_hbm, kept),
                 (q_hbm, q_ref),
                 (g_hbm, g_ref),
                 (gain_hbm, gain_ref),
@@ -132,8 +134,8 @@
     ]
     for load in loads:
         load.start()
-    loads[0].wait()
-    loads[1].wait()
+    for load in loads[:3]:
+        load.wait()
 
     for level in range(LEVELS):
         for slot in range(KEEP):
@@ -169,7 +171,7 @@
         for level in (2, 0, 1):
             kv_copy(level, c).start()
 
-    for load in loads[2:]:
+    for load in loads[3:]:
         load.wait()
     start1 = lengths[0]
     start2 = lengths[0] + lengths[1]
@@ -457,40 +459,54 @@
 
 
 def finish(
-    kept, lo_in, dq_in, part_in, gr_in, gg_in, lo_ref, dq_ref, dk_ref, dv_ref, gg_ref
+    kept, lo_in, dq_in, part_in, gr_in, gg_in, lo_ref, dq_ref, dk_ref, dv_ref, gg_ref, dk, dv, sems
 ):
     me = lax.axis_index("seq")
-    step = pl.program_id(0)
-    lo_ref[...] = lo_in[...]
-    dq_ref[...] = dq_in[...]
     gg_ref[...] = gg_in[...]
-    for i in range(TILE // BLOCK):
-        rows = slice(i * BLOCK, (i + 1) * BLOCK)
-        block = step * (TILE // BLOCK) + i
-        total = part_in[rows, :]
-        dk = [total[:, h * DH : (h + 1) * DH] for h in range(HEADS_DEV)]
-        dv = [total[:, COLS + h * DH : COLS + (h + 1) * DH] for h in range(HEADS_DEV)]
-        for level in range(2):
-            found = jnp.int32(-1)
-            for slot in range(KEEP):
-                found = jnp.where(kept[level, slot, me] == block, jnp.int32(slot), found)
-            used = jnp.minimum(found + 1, 1).astype(F32)
+    copies = []
+
+    def send(src, dst, i, lane):
+        rows = pl.ds(i * TILE, TILE)
+        copy = pltpu.make_async_copy(src.at[rows], dst.at[rows], sems.at[lane, i])
+        copy.start()
+        copies.append(copy)
+
+    for i in range(TOK // TILE):
+        send(lo_in, lo_ref, i, 0)
+        send(dq_in, dq_ref, i, 1)
+    for i in range(TOK // TILE):
+        for b in range(i * (TILE // BLOCK), (i + 1) * (TILE // BLOCK)):
+            rows = slice(b * BLOCK, (b + 1) * BLOCK)
+            total = part_in[rows, :]
+            key = [total[:, h * DH : (h + 1) * DH] for h in range(HEADS_DEV)]
+            value = [total[:, COLS + h * DH : COLS + (h + 1) * DH] for h in range(HEADS_DEV)]
+            for level in range(2):
+                found = jnp.int32(-1)
+                for slot in range(KEEP):
+                    found = jnp.where(kept[level, slot, me] == b, jnp.int32(slot), found)
+                used = jnp.minimum(found + 1, 1).astype(F32)
+                for h in range(HEADS_DEV):
+                    part = gr_in[level, h, jnp.maximum(found, 0)].astype(F32) * used
+                    key[h] = key[h] + part[:, 0:DH]
+                    value[h] = value[h] + part[:, DH:]
             for h in range(HEADS_DEV):
-                part = gr_in[level, h, jnp.maximum(found, 0)].astype(F32) * used
-                dk[h] = dk[h] + part[:, 0:DH]
-                dv[h] = dv[h] + part[:, DH:]
-        for h in range(HEADS_DEV):
-            dk_ref[rows, h * DH : (h + 1) * DH] = dk[h].astype(BF16)
-            dv_ref[rows, h * DH : (h + 1) * DH] = dv[h].astype(BF16)
+                dk[rows, h * DH : (h + 1) * DH] = key[h].astype(BF16)
+                dv[rows, h * DH : (h + 1) * DH] = value[h].astype(BF16)
+        send(dk, dk_ref, i, 2)
+        send(dv, dv_ref, i, 3)
+    for copy in copies:
+        copy.wait()
 
 
 def local(query_rows, key_rows, value_rows, norm_gain, grad_out, doc_lengths, kept_blocks):
     vmem = pl.BlockSpec(memory_space=pltpu.VMEM)
     smem = pl.BlockSpec(memory_space=pltpu.SMEM)
-    hbm = pl.BlockSpec(memory_space=pl.ANY)
+    hbm = pl.BlockSpec(memory_space=pltpu.HBM)
+    some = pl.BlockSpec(memory_space=pl.ANY)
     rows = jax.ShapeDtypeStruct((TOK, COLS), BF16)
     dma = pltpu.SemaphoreType.DMA
     scratch = [
+        pltpu.SMEM((LEVELS, KEEP, N_SEQ), jnp.int32),
         pltpu.VMEM((TOK, COLS), BF16),
         pltpu.VMEM((TOK // BLOCK, BLOCK, COLS), BF16),
         pltpu.VMEM((TOK // BLOCK, BLOCK, COLS), BF16),
@@ -535,53 +551,53 @@
         dma((N_HEAD,)),
         dma((4,)),
         dma((4,)),
-        dma((5,)),
+        dma((6,)),
     ]
     kept = jnp.transpose(kept_blocks, (1, 2, 0))
     gain_row = jax.ShapeDtypeStruct((1, COLS), F32)
     lo, dq, part, returned, gain = pl.pallas_call(
         kernel,
         out_shape=[
-            rows,
-            rows,
-            jax.ShapeDtypeStruct((TOK, 2 * COLS), F32),
-            jax.ShapeDtypeStruct((2, HEADS_DEV, KEEP, BLOCK, 2 * DH), BF16),
-            gain_row,
+            pltpu.VMEM((TOK, COLS), BF16),
+            pltpu.VMEM((TOK, COLS), BF16),
+            pltpu.VMEM((TOK, 2 * COLS), F32),
+            pltpu.VMEM((2, HEADS_DEV, KEEP, BLOCK, 2 * DH), BF16),
+            pltpu.VMEM((1, COLS), F32),
         ],
-        in_specs=[smem, smem] + [hbm] * 5,
-        out_specs=[hbm] * 4 + [vmem],
+        in_specs=[hbm, smem] + [hbm] * 5,
+        out_specs=[some] * 4 + [vmem],
         scratch_shapes=scratch,
         compiler_params=pltpu.CompilerParams(
-            collective_id=0, has_side_effects=True, vmem_limit_bytes=56 * 1024 * 1024
+            collective_id=0, has_side_effects=True, vmem_limit_bytes=44 * 1024 * 1024
         ),
         name="attention",
     )(
-        kept,
-        doc_lengths,
-        query_rows,
-        key_rows.reshape(TOK // BLOCK, BLOCK, COLS),
-        value_rows.reshape(TOK // BLOCK, BLOCK, COLS),
-        norm_gain.reshape(1, COLS),
-        grad_out,
+        *(
+            pltpu.with_memory_space_constraint(x, pltpu.HBM)
+            for x in (
+                kept,
+                doc_lengths,
+                query_rows,
+                key_rows.reshape(TOK // BLOCK, BLOCK, COLS),
+                value_rows.reshape(TOK // BLOCK, BLOCK, COLS),
+                norm_gain.reshape(1, COLS),
+                grad_out,
+            )
+        )
     )
-    tile = pl.BlockSpec((TILE, COLS), lambda i: (i, 0))
-    gain_spec = pl.BlockSpec((1, COLS), lambda i: (0, 0))
     lo, dq, dk, dv, gain = pl.pallas_call(
         finish,
-        grid=(TOK // TILE,),
         out_shape=[rows, rows, rows, rows, gain_row],
-        in_specs=[
-            smem,
-            tile,
-            tile,
-            pl.BlockSpec((TILE, 2 * COLS), lambda i: (i, 0)),
-            pl.BlockSpec(returned.shape, lambda i: (0, 0, 0, 0, 0)),
-            gain_spec,
+        in_specs=[smem] + [vmem] * 5,
+        out_specs=[hbm] * 4 + [vmem],
+        scratch_shapes=[
+            pltpu.VMEM((TOK, COLS), BF16),
+            pltpu.VMEM((TOK, COLS), BF16),
+            dma((4, TOK // TILE)),
         ],
-        out_specs=[tile, tile, tile, tile, gain_spec],
-        compiler_params=pltpu.CompilerParams(vmem_limit_bytes=60 * 1024 * 1024),
+        compiler_params=pltpu.CompilerParams(vmem_limit_bytes=12 * 1024 * 1024),
         name="finish",
-    )(kept, lo, dq, part, returned, gain)
+    )(pltpu.with_memory_space_constraint(kept, pltpu.HBM), lo, dq, part, returned, gain)
     return lo, dq, dk, dv, gain.reshape(COLS)
 
 

time: 72.7 us -> 70 us (0.963)
  Pallas kernels: 71.8 us -> 69.1 us
    pallas_call x2, Pallas kernels: 71.8 us -> 69.1 us  [the longest x1 66.3 us: local(): pl.pallas_call(kernel, out_shape=[pltpu.VMEM((TOK, COLS), BF16), pltpu.VM...]
where the time goes in v2:
time: 70 us; the launch traced here: 69.8 us
  Pallas kernels  69.1 us (99%)
    pallas_call x1, Pallas kernels, local(): pl.pallas_call(kernel, out_shape=[pltpu.VMEM((TOK, COLS), BF16), pltpu.VM...  66.3 us
    pallas_call x1, Pallas kernels, local(): pl.pallas_call(finish, out_shape=[rows, rows, rows, rows, gain_row], in_s...  2.86 us

profile of v2, /device:TPU:0, one launch (start us, length us, event | category | flops | bytes accessed | tf_op | source)
XLA Modules:
  0.0 69.8 jit_solution(2607419707095565092)
XLA Ops:
  0.6 66.3 %attention.1 = (bf16[1024,256]{1,0:T(8,128)(2,1)S(1)}, bf16[1024,256]{1,0:T(8,128)(2,1)S(1)}, f32[1024,512]{1,0:T(8,128)S(1)}, bf16[2,2,8,64,256]{4,3,2,1,0:T(8,128)(2,1)S(1)}, f32[1,256]{1,0:T(1,128)S(1)}) custom-call(s32[3,8,16]{2,1,0:T(8,128)} %bitcast.7, s32[3]{0:T(128)} %lengths.1, bf16[1024,256]{1,0:T(8,128)(2,1)} %q_hbm.1, ...), custom_call_target="tpu_custom_call" | custom-call | tf_op jit(solution)/shard_map/attention/pallas_call | solution.py:558
  66.9 2.9 %finish.1 = (bf16[1024,256]{1,0:T(8,128)(2,1)}, bf16[1024,256]{1,0:T(8,128)(2,1)}, bf16[1024,256]{1,0:T(8,128)(2,1)}, bf16[1024,256]{1,0:T(8,128)(2,1)}, f32[1,256]{1,0:T(1,128)}) custom-call(s32[3,8,16]{2,1,0:T(8,128)} %bitcast.8, bf16[1024,256]{1,0:T(8,128)(2,1)S(1)} %get-tuple-element.15.lo_in, bf16[1024,256]{1,0:T(8,128)(2,1)S(1)} %get-tuple-element.16.dq_in, ...), custom_call_target="tpu_custom_call" | custom-call | tf_op jit(solution)/shard_map/finish/pallas_call | solution.py:588

commit v3 on v2

--- a/solution.py
+++ b/solution.py
@@ -91,6 +91,7 @@
     gt,
     gc,
     st,
+    early,
     res,
     dot_,
     delta,
@@ -119,23 +120,19 @@
             barrier, inc=1, device_id=(me, lax.rem(col + d, N_HEAD)), device_id_type=MESH
         )
 
-    loads = [
-        pltpu.make_async_copy(src, dst, io.at[i])
-        for i, (src, dst) in enumerate(
-            (
-                (k_hbm, k_ref),
-                (v_hbm, v_ref),
-                (kept_hbm, kept),
-                (q_hbm, q_ref),
-                (g_hbm, g_ref),
-                (gain_hbm, gain_ref),
-            )
-        )
-    ]
-    for load in loads:
-        load.start()
-    for load in loads[:3]:
-        load.wait()
+    def load(src, dst, pieces, first):
+        size = src.shape[0] // pieces
+        copies = []
+        for i in range(pieces):
+            rows = pl.ds(i * size, size)
+            copies.append(pltpu.make_async_copy(src.at[rows], dst.at[rows], io.at[first + i]))
+            copies[-1].start()
+        return copies
+
+    loads = load(k_hbm, k_ref, 4, 0) + load(v_hbm, v_ref, 4, 4) + load(kept_hbm, kept, 1, 8)
+    later = load(q_hbm, q_ref, 4, 9) + load(g_hbm, g_ref, 4, 13) + load(gain_hbm, gain_ref, 1, 17)
+    for copy in loads:
+        copy.wait()
 
     for level in range(LEVELS):
         for slot in range(KEEP):
@@ -155,24 +152,23 @@
             device_id_type=MESH,
         )
 
-    def gr_copy(level, c, h):
-        blocks = pl.ds(c * (CHUNK // BLOCK), CHUNK // BLOCK)
+    def gr_copy(level, h):
         dst = gr_in2 if level == 2 else gr_hbm.at[level]
         return pltpu.make_async_remote_copy(
-            src_ref=gr_out.at[level, h, blocks],
-            dst_ref=dst.at[h, blocks],
-            send_sem=gr_ss.at[level, c, h],
-            recv_sem=gr_rs.at[level, c, h],
+            src_ref=gr_out.at[level, h],
+            dst_ref=dst.at[h],
+            send_sem=gr_ss.at[level, h],
+            recv_sem=gr_rs.at[level, h],
             device_id=(flipped(me, level_bit(level)), col),
             device_id_type=MESH,
         )
 
     for c in range(NCH):
-        for level in (2, 0, 1):
+        for level in (1, 0, 2):
             kv_copy(level, c).start()
 
-    for load in loads[3:]:
-        load.wait()
+    for copy in later:
+        copy.wait()
     start1 = lengths[0]
     start2 = lengths[0] + lengths[1]
 
@@ -240,6 +236,23 @@
         cols = slice(t * TILE, (t + 1) * TILE)
         gt[:, cols] = jnp.transpose(g_ref[cols, :].astype(F32))
 
+    for i in range(TOK // DH):
+        scaled = gt[:, i * DH : (i + 1) * DH] * gc[...]
+        early[0, i : i + 1, :] = jnp.sum(scaled, axis=0, keepdims=True)
+
+    def row_copy(buffer, lane, d):
+        return pltpu.make_async_remote_copy(
+            src_ref=buffer.at[0],
+            dst_ref=buffer.at[d],
+            send_sem=st_ss.at[lane, d],
+            recv_sem=st_rs.at[lane, d],
+            device_id=(me, lax.rem(col + d, N_HEAD)),
+            device_id_type=MESH,
+        )
+
+    for d in range(1, N_HEAD):
+        row_copy(early, 0, d).start()
+
     @pl.loop(0, TOK // BLOCK)
     def _(b):
         found = jnp.int32(-1)
@@ -250,7 +263,7 @@
 
     @pl.loop(0, LEVELS * NCH)
     def _(t):
-        level = lax.rem(t + 2, 3)
+        level = 2 - lax.rem(t, 3)
         c = t // 3
         kv_copy(level, c).wait()
         rows = pl.ds(pl.multiple_of(c * CHUNK, CHUNK), CHUNK)
@@ -288,23 +301,14 @@
         scaled = gt[:, qs] * gc[...]
         st[0, i : i + 1, 0:128] = mean
         st[0, i : i + 1, 128:256] = jnp.sum(centred * centred, axis=0, keepdims=True)
-        st[0, i : i + 1, 256:384] = jnp.sum(scaled, axis=0, keepdims=True)
-        st[0, i : i + 1, 384:512] = jnp.sum(scaled * centred, axis=0, keepdims=True)
-
-    def st_copy(d):
-        return pltpu.make_async_remote_copy(
-            src_ref=st.at[0],
-            dst_ref=st.at[d],
-            send_sem=st_ss.at[d],
-            recv_sem=st_rs.at[d],
-            device_id=(me, lax.rem(col + d, N_HEAD)),
-            device_id_type=MESH,
-        )
-
+        st[0, i : i + 1, 256:384] = jnp.sum(scaled * centred, axis=0, keepdims=True)
+
+    for d in (4, 3, 5, 2, 6, 1, 7):
+        row_copy(st, 1, d).start()
     for d in range(1, N_HEAD):
-        st_copy(d).start()
+        row_copy(early, 0, d).wait()
     for d in range(1, N_HEAD):
-        st_copy(d).wait()
+        row_copy(st, 1, d).wait()
 
     mean = st[0, :, 0:128]
     for d in range(1, N_HEAD):
@@ -316,8 +320,8 @@
     for d in range(N_HEAD):
         off = st[d, :, 0:128] - mean
         square = square + (st[d, :, 128:256] + COLS * (off * off))
-        plain = plain + st[d, :, 256:384]
-        cross = cross + (st[d, :, 384:512] + off * st[d, :, 256:384])
+        plain = plain + early[d]
+        cross = cross + (st[d, :, 256:384] + off * early[d])
     inv_std = lax.rsqrt(square * (1.0 / WIDTH) + NORM_EPS)
     res[:, 0:128] = mean
     res[:, 128:256] = inv_std
@@ -338,14 +342,20 @@
         for h in range(HEADS_DEV):
             delta[h, :, qs] = jnp.sum(both[h * DH : (h + 1) * DH], axis=0, keepdims=True)
 
-    def back(h, qs, m, v, kt, p):
-        factor = jnp.exp2((m - m_run[h, :, qs]) * coef) * inv_l[h, :, qs]
-        do = (dot_[h * DH : (h + 1) * DH, qs].astype(F32) * factor).astype(BF16)
+    def back(h, qs, parts, v, kt):
+        probs = jnp.concatenate(
+            [
+                p.astype(F32) * (jnp.exp2((m - m_run[h, :, qs]) * coef) * inv_l[h, :, qs])
+                for p, m in parts
+            ],
+            axis=0,
+        )
+        do = dot_[h * DH : (h + 1) * DH, qs]
         dp = dot(v, do, 1, 0)
-        ds = (p.astype(F32) * (dp - factor * delta[h, :, qs])).astype(BF16)
+        ds = (probs * (dp - delta[h, :, qs])).astype(BF16)
         dq = dot(kt, ds, 1, 0)
         dk = dot(ds, qa[h, qs, 0:DH], 1, 0)
-        dv = dot(p, do, 1, 1)
+        dv = dot(probs.astype(BF16), do, 1, 1)
         return dq, dk, dv
 
     dqt[...] = jnp.zeros_like(dqt)
@@ -370,34 +380,35 @@
 
     gg_copy(0).start()
 
-    @pl.loop(0, LEVELS * NCH)
+    @pl.loop(0, LEVELS)
     def _(t):
-        level = lax.rem(t, 3)
-        c = t // 3
-        rows = pl.ds(pl.multiple_of(c * CHUNK, CHUNK), CHUNK)
+        level = lax.rem(4 - t, 3)
         for h in range(HEADS_DEV):
             hs = slice(h * DH, (h + 1) * DH)
-            v = kv_in[level, rows, COLS + h * DH : COLS + (h + 1) * DH]
-            kt = kt_far[level, hs, rows]
-            dk_sum = jnp.zeros((CHUNK, DH), F32)
-            dv_sum = jnp.zeros((CHUNK, DH), F32)
+            v = kv_in[level, :, COLS + h * DH : COLS + (h + 1) * DH]
+            kt = kt_far[level, hs, :]
+            dk_sum = jnp.zeros((KEPT, DH), F32)
+            dv_sum = jnp.zeros((KEPT, DH), F32)
             for j in range(TOK // TILE):
                 qs = slice(j * TILE, (j + 1) * TILE)
-                dq, dk, dv = back(h, qs, m_far[level, c, h, :, qs], v, kt, p_far[level, h, rows, qs])
+                parts = [
+                    (p_far[level, h, c * CHUNK : (c + 1) * CHUNK, qs], m_far[level, c, h, :, qs])
+                    for c in range(NCH)
+                ]
+                dq, dk, dv = back(h, qs, parts, v, kt)
                 dqt[hs, qs] += dq
                 dk_sum = dk_sum + dk
                 dv_sum = dv_sum + dv
-            blocks = pl.ds(c * (CHUNK // BLOCK), CHUNK // BLOCK)
-            shape = (CHUNK // BLOCK, BLOCK, DH)
-            gr_out[level, h, blocks, :, 0:DH] = (dk_sum * SCALE).astype(BF16).reshape(shape)
-            gr_out[level, h, blocks, :, DH:] = dv_sum.astype(BF16).reshape(shape)
+            shape = (KEEP, BLOCK, DH)
+            gr_out[level, h, :, :, 0:DH] = (dk_sum * SCALE).astype(BF16).reshape(shape)
+            gr_out[level, h, :, :, DH:] = dv_sum.astype(BF16).reshape(shape)
             if h == 0:
                 pl.when(t == 0)(lambda: gg_end(0))
                 pl.when(t == 1)(lambda: gg_end(2))
             else:
                 pl.when(t == 0)(lambda: gg_end(1))
             for one in range(LEVELS):
-                pl.when(level == one)(lambda one=one, h=h: gr_copy(one, c, h).start())
+                pl.when(level == one)(lambda one=one, h=h: gr_copy(one, h).start())
 
     for i in range(TOK // DH):
         qs = slice(i * DH, (i + 1) * DH)
@@ -418,7 +429,7 @@
             dv_sum = jnp.zeros((SEG, DH), F32)
             for j in range(SEG // TILE):
                 qs = pl.ds(pl.multiple_of(t * SEG + j * TILE, TILE), TILE)
-                dq, dk, dv = back(h, qs, m_loc[h, :, qs], v, kt, p_loc[h, :, qs])
+                dq, dk, dv = back(h, qs, [(p_loc[h, :, qs], m_loc[h, :, qs])], v, kt)
                 dqt[hs, qs] += dq
                 dk_sum = dk_sum + dk
                 dv_sum = dv_sum + dv
@@ -433,9 +444,8 @@
     gg_end(3)
     gg_ref[...] = gsum[8, 0:1, :]
 
-    for c in range(NCH):
-        for h in range(HEADS_DEV):
-            gr_copy(2, c, h).wait()
+    for h in range(HEADS_DEV):
+        gr_copy(2, h).wait()
 
     @pl.loop(0, TOK // BLOCK)
     def _(b):
@@ -449,10 +459,9 @@
 
     part_copy = pltpu.make_async_copy(dkv, part_hbm, io.at[2])
     part_copy.start()
-    for c in range(NCH):
-        for level in range(2):
-            for h in range(HEADS_DEV):
-                gr_copy(level, c, h).wait()
+    for level in range(2):
+        for h in range(HEADS_DEV):
+            gr_copy(level, h).wait()
     lo_copy.wait()
     dq_copy.wait()
     part_copy.wait()
@@ -535,7 +544,8 @@
         pltpu.VMEM((COLS, TOK), F32),
         pltpu.VMEM((COLS, TOK), F32),
         pltpu.VMEM((COLS, DH), F32),
-        pltpu.VMEM((N_HEAD, 8, 512), F32),
+        pltpu.VMEM((N_HEAD, 8, 384), F32),
+        pltpu.VMEM((N_HEAD, 8, DH), F32),
         pltpu.VMEM((8, 512), F32),
         pltpu.VMEM((COLS, TOK), BF16),
         pltpu.VMEM((HEADS_DEV, 1, TOK), F32),
@@ -545,13 +555,13 @@
         pltpu.SMEM((TOK // BLOCK,), jnp.int32),
         dma((LEVELS, NCH)),
         dma((LEVELS, NCH)),
-        dma((LEVELS, NCH, HEADS_DEV)),
-        dma((LEVELS, NCH, HEADS_DEV)),
-        dma((N_HEAD,)),
-        dma((N_HEAD,)),
+        dma((LEVELS, HEADS_DEV)),
+        dma((LEVELS, HEADS_DEV)),
+        dma((2, N_HEAD)),
+        dma((2, N_HEAD)),
         dma((4,)),
         dma((4,)),
-        dma((6,)),
+        dma((18,)),
     ]
     kept = jnp.transpose(kept_blocks, (1, 2, 0))
     gain_row = jax.ShapeDtypeStruct((1, COLS), F32)

time: 70 us -> 67.6 us (0.966)
  Pallas kernels: 69.1 us -> 66.8 us
    pallas_call x1, Pallas kernels: 66.3 us -> 63.9 us  [local(): pl.pallas_call(kernel, out_shape=[pltpu.VMEM((TOK, COLS), BF16), pltpu.VM...]
where the time goes in v3:
time: 67.6 us; the launch traced here: 67.4 us
  Pallas kernels  66.8 us (99%)
    pallas_call x1, Pallas kernels, local(): pl.pallas_call(kernel, out_shape=[pltpu.VMEM((TOK, COLS), BF16), pltpu.VM...  63.9 us
    pallas_call x1, Pallas kernels, local(): pl.pallas_call(finish, out_shape=[rows, rows, rows, rows, gain_row], in_s...  2.86 us

profile of v3, /device:TPU:0, one launch (start us, length us, event | category | flops | bytes accessed | tf_op | source)
XLA Modules:
  0.0 67.4 jit_solution(2411414956021293220)
XLA Ops:
  0.6 63.9 %attention.1 = (bf16[1024,256]{1,0:T(8,128)(2,1)S(1)}, bf16[1024,256]{1,0:T(8,128)(2,1)S(1)}, f32[1024,512]{1,0:T(8,128)S(1)}, bf16[2,2,8,64,256]{4,3,2,1,0:T(8,128)(2,1)S(1)}, f32[1,256]{1,0:T(1,128)S(1)}) custom-call(s32[3,8,16]{2,1,0:T(8,128)} %bitcast.7, s32[3]{0:T(128)} %lengths.1, bf16[1024,256]{1,0:T(8,128)(2,1)} %q_hbm.1, ...), custom_call_target="tpu_custom_call" | custom-call | tf_op jit(solution)/shard_map/attention/pallas_call | solution.py:568
  64.5 2.9 %finish.1 = (bf16[1024,256]{1,0:T(8,128)(2,1)}, bf16[1024,256]{1,0:T(8,128)(2,1)}, bf16[1024,256]{1,0:T(8,128)(2,1)}, bf16[1024,256]{1,0:T(8,128)(2,1)}, f32[1,256]{1,0:T(1,128)}) custom-call(s32[3,8,16]{2,1,0:T(8,128)} %bitcast.8, bf16[1024,256]{1,0:T(8,128)(2,1)S(1)} %get-tuple-element.15.lo_in, bf16[1024,256]{1,0:T(8,128)(2,1)S(1)} %get-tuple-element.16.dq_in, ...), custom_call_target="tpu_custom_call" | custom-call | tf_op jit(solution)/shard_map/finish/pallas_call | solution.py:598

commit v4 on v3

--- a/solution.py
+++ b/solution.py
@@ -18,6 +18,7 @@
 NCH = KEPT // CHUNK
 TILE = 256
 WIDTH = 2048
+HALVES = 2
 HEADS_DEV = 2
 COLS = HEADS_DEV * DH
 N_SEQ = 16
@@ -99,6 +100,18 @@
     dkv,
     gsum,
     inv_slot,
+    mq_far,
+    mk_own,
+    q_in,
+    do_in,
+    rows_out,
+    rows_in,
+    q_ss,
+    q_rs,
+    do_ss,
+    do_rs,
+    ro_ss,
+    ro_rs,
     kv_ss,
     kv_rs,
     gr_ss,
@@ -113,8 +126,9 @@
     col = lax.axis_index("head")
 
     barrier = pltpu.get_barrier_semaphore()
-    for bit in (1, 2, 4, 8):
-        pl.semaphore_signal(barrier, inc=1, device_id=(flipped(me, bit), col), device_id_type=MESH)
+    beside = flipped(flipped(me, 1), 2)
+    for other in [flipped(me, bit) for bit in (1, 2, 4, 8)] + [beside]:
+        pl.semaphore_signal(barrier, inc=1, device_id=(other, col), device_id_type=MESH)
     for d in range(1, N_HEAD):
         pl.semaphore_signal(
             barrier, inc=1, device_id=(me, lax.rem(col + d, N_HEAD)), device_id_type=MESH
@@ -139,7 +153,7 @@
             block = jnp.maximum(kept[level, slot, me], 0)
             kv_out[level, slot * BLOCK : (slot + 1) * BLOCK, 0:COLS] = k_ref[block]
             kv_out[level, slot * BLOCK : (slot + 1) * BLOCK, COLS:] = v_ref[block]
-    pl.semaphore_wait(barrier, 4 + N_HEAD - 1)
+    pl.semaphore_wait(barrier, 5 + N_HEAD - 1)
 
     def kv_copy(level, c):
         rows = pl.ds(pl.multiple_of(c * CHUNK, CHUNK), CHUNK)
@@ -160,6 +174,38 @@
             send_sem=gr_ss.at[level, h],
             recv_sem=gr_rs.at[level, h],
             device_id=(flipped(me, level_bit(level)), col),
+            device_id_type=MESH,
+        )
+
+    def q_copy(hop, c):
+        qs = pl.ds(c * (TOK // HALVES), TOK // HALVES)
+        return pltpu.make_async_remote_copy(
+            src_ref=q_in.at[0, qs] if hop else q_ref.at[qs, pl.ds(DH, DH)],
+            dst_ref=q_in.at[hop, qs],
+            send_sem=q_ss.at[hop, c],
+            recv_sem=q_rs.at[hop, c],
+            device_id=(beside if hop else flipped(me, 1), col),
+            device_id_type=MESH,
+        )
+
+    def do_copy(hop, c):
+        qs = pl.ds(c * (TOK // HALVES), TOK // HALVES)
+        return pltpu.make_async_remote_copy(
+            src_ref=do_in.at[0, :, qs] if hop else dot_.at[pl.ds(DH, DH), qs],
+            dst_ref=do_in.at[hop, :, qs],
+            send_sem=do_ss.at[hop, c],
+            recv_sem=do_rs.at[hop, c],
+            device_id=(beside if hop else flipped(me, 1), col),
+            device_id_type=MESH,
+        )
+
+    def rows_copy(level):
+        return pltpu.make_async_remote_copy(
+            src_ref=rows_out,
+            dst_ref=rows_in.at[level],
+            send_sem=ro_ss.at[level],
+            recv_sem=ro_rs.at[level],
+            device_id=(flipped(me, 1 << level), col),
             device_id_type=MESH,
         )
 
@@ -197,6 +243,19 @@
                 same | (lane >= 3), 0.0, -BIG
             ).astype(BF16)
 
+    for level in range(2):
+        partner = flipped(me, level_bit(level))
+        for b in range(TOK // BLOCK):
+            same = doc_of(partner * TOK + b * BLOCK + row) == lane
+            mq_far[level, b * BLOCK : (b + 1) * BLOCK, :] = jnp.where(same, 1.0, 0.0).astype(BF16)
+        for slot in range(KEEP):
+            listed = kept[level, slot, me]
+            docs = doc_of(me * TOK + jnp.maximum(listed, 0) * BLOCK + row)
+            docs = docs - 3 * jnp.minimum(listed, 0)
+            mk_own[level, slot * BLOCK : (slot + 1) * BLOCK, :] = jnp.where(
+                (docs == lane) | (lane >= 3), 0.0, -BIG
+            ).astype(BF16)
+
     ones = jnp.ones((16, TOK), BF16)
     for h in range(HEADS_DEV):
         vt_loc[h, DH:, :] = ones
@@ -266,6 +325,12 @@
         level = 2 - lax.rem(t, 3)
         c = t // 3
         kv_copy(level, c).wait()
+
+        @pl.when(t == LEVELS * NCH - 1)
+        def _():
+            for half in range(HALVES):
+                q_copy(0, half).start()
+
         rows = pl.ds(pl.multiple_of(c * CHUNK, CHUNK), CHUNK)
         kt_far[level, :, rows] = turned(kv_in[level, rows, 0:COLS])
         vt = turned(kv_in[level, rows, COLS:])
@@ -341,8 +406,11 @@
         both = do.astype(F32) * at[:, qs]
         for h in range(HEADS_DEV):
             delta[h, :, qs] = jnp.sum(both[h * DH : (h + 1) * DH], axis=0, keepdims=True)
-
-    def back(h, qs, parts, v, kt):
+        log_l = jnp.log(acc[1, DH : DH + 1, qs])
+        rows_out[i : i + 1, 0:DH] = m_run[1, :, qs] + log_l * (1.0 / SCALE)
+        rows_out[i : i + 1, DH:] = delta[1, :, qs]
+
+    def back(h, qs, parts, v, kt, whole=True):
         probs = jnp.concatenate(
             [
                 p.astype(F32) * (jnp.exp2((m - m_run[h, :, qs]) * coef) * inv_l[h, :, qs])
@@ -354,6 +422,8 @@
         dp = dot(v, do, 1, 0)
         ds = (probs * (dp - delta[h, :, qs])).astype(BF16)
         dq = dot(kt, ds, 1, 0)
+        if not whole:
+            return dq, None, None
         dk = dot(ds, qa[h, qs, 0:DH], 1, 0)
         dv = dot(probs.astype(BF16), do, 1, 1)
         return dq, dk, dv
@@ -363,52 +433,80 @@
     gsum[0] = jnp.broadcast_to(jnp.sum(jnp.transpose(gain_part), axis=0, keepdims=True), (8, COLS))
 
     def gg_copy(stage):
+        flip, src, dst = ((1, 0, 1), (2, 0, 2), (3, 0, 3), (4, 4, 5), (8, 6, 7))[stage]
         return pltpu.make_async_remote_copy(
-            src_ref=gsum.at[2 * stage],
-            dst_ref=gsum.at[2 * stage + 1],
+            src_ref=gsum.at[src],
+            dst_ref=gsum.at[dst],
             send_sem=gg_ss.at[stage],
             recv_sem=gg_rs.at[stage],
-            device_id=(flipped(me, 1 << stage), col),
+            device_id=(beside if flip == 3 else flipped(me, flip), col),
             device_id_type=MESH,
         )
 
-    def gg_end(stage):
-        gg_copy(stage).wait()
-        gsum[2 * stage + 2] = gsum[2 * stage] + gsum[2 * stage + 1]
-        if stage < 3:
-            gg_copy(stage + 1).start()
-
-    gg_copy(0).start()
-
-    @pl.loop(0, LEVELS)
-    def _(t):
-        level = lax.rem(4 - t, 3)
-        for h in range(HEADS_DEV):
-            hs = slice(h * DH, (h + 1) * DH)
-            v = kv_in[level, :, COLS + h * DH : COLS + (h + 1) * DH]
-            kt = kt_far[level, hs, :]
-            dk_sum = jnp.zeros((KEPT, DH), F32)
-            dv_sum = jnp.zeros((KEPT, DH), F32)
-            for j in range(TOK // TILE):
-                qs = slice(j * TILE, (j + 1) * TILE)
-                parts = [
-                    (p_far[level, h, c * CHUNK : (c + 1) * CHUNK, qs], m_far[level, c, h, :, qs])
-                    for c in range(NCH)
-                ]
-                dq, dk, dv = back(h, qs, parts, v, kt)
-                dqt[hs, qs] += dq
+    for stage in range(3):
+        gg_copy(stage).start()
+    for level in range(2):
+        rows_copy(level).start()
+    for c in range(HALVES):
+        do_copy(0, c).start()
+
+    def back_level(level, h, whole):
+        hs = slice(h * DH, (h + 1) * DH)
+        v = kv_in[level, :, COLS + h * DH : COLS + (h + 1) * DH]
+        kt = kt_far[level, hs, :]
+        dk_sum = jnp.zeros((KEPT, DH), F32)
+        dv_sum = jnp.zeros((KEPT, DH), F32)
+        for j in range(TOK // TILE):
+            qs = slice(j * TILE, (j + 1) * TILE)
+            parts = [
+                (p_far[level, h, c * CHUNK : (c + 1) * CHUNK, qs], m_far[level, c, h, :, qs])
+                for c in range(NCH)
+            ]
+            dq, dk, dv = back(h, qs, parts, v, kt, whole)
+            dqt[hs, qs] += dq
+            if whole:
                 dk_sum = dk_sum + dk
                 dv_sum = dv_sum + dv
-            shape = (KEEP, BLOCK, DH)
-            gr_out[level, h, :, :, 0:DH] = (dk_sum * SCALE).astype(BF16).reshape(shape)
-            gr_out[level, h, :, :, DH:] = dv_sum.astype(BF16).reshape(shape)
-            if h == 0:
-                pl.when(t == 0)(lambda: gg_end(0))
-                pl.when(t == 1)(lambda: gg_end(2))
-            else:
-                pl.when(t == 0)(lambda: gg_end(1))
-            for one in range(LEVELS):
-                pl.when(level == one)(lambda one=one, h=h: gr_copy(one, h).start())
+        if whole:
+            keep_grads(level, h, dk_sum, dv_sum)
+
+    def keep_grads(level, h, dk_sum, dv_sum):
+        shape = (KEEP, BLOCK, DH)
+        gr_out[level, h, :, :, 0:DH] = (dk_sum * SCALE).astype(BF16).reshape(shape)
+        gr_out[level, h, :, :, DH:] = dv_sum.astype(BF16).reshape(shape)
+
+    @pl.loop(0, 2)
+    def _(t):
+        level = 1 - t
+        back_level(level, 0, True)
+        for one in range(2):
+
+            @pl.when(level == one)
+            def _():
+                if one == 1:
+                    for c in range(HALVES):
+                        q_copy(0, c).wait()
+                        q_copy(1, c).start()
+                else:
+                    for stage in range(3):
+                        gg_copy(stage).wait()
+                    gsum[4] = (gsum[0] + gsum[1]) + (gsum[2] + gsum[3])
+                    gg_copy(3).start()
+                gr_copy(one, 0).start()
+
+    for h in range(HEADS_DEV):
+        back_level(2, h, True)
+        do_copy(0, h).wait()
+        do_copy(1, h).start()
+        if h == 0:
+            gg_copy(3).wait()
+            gsum[6] = gsum[4] + gsum[5]
+            gg_copy(4).start()
+        gr_copy(2, h).start()
+
+    @pl.loop(0, 2)
+    def _(level):
+        back_level(level, 1, False)
 
     for i in range(TOK // DH):
         qs = slice(i * DH, (i + 1) * DH)
@@ -441,8 +539,45 @@
         dq_ref[cols, :] = jnp.transpose(dqt[:, cols] * SCALE).astype(BF16)
     dq_copy = pltpu.make_async_copy(dq_ref, dq_hbm, io.at[1])
     dq_copy.start()
-    gg_end(3)
-    gg_ref[...] = gsum[8, 0:1, :]
+    gg_copy(4).wait()
+    gg_ref[...] = gsum[6, 0:1, :] + gsum[7, 0:1, :]
+
+    @pl.loop(0, 2)
+    def _(level):
+        for one in range(2):
+
+            @pl.when(level == one)
+            def _():
+                rows_copy(one).wait()
+                if one == 1:
+                    for c in range(HALVES):
+                        q_copy(1, c).wait()
+                        do_copy(1, c).wait()
+
+        ka = jnp.concatenate([kv_out[level, :, DH:COLS], mk_own[level]], axis=1)
+        v = kv_out[level, :, COLS + DH :]
+        dk_sum = jnp.zeros((KEPT, DH), F32)
+        dv_sum = jnp.zeros((KEPT, DH), F32)
+        for j in range(TOK // TILE):
+            qs = slice(j * TILE, (j + 1) * TILE)
+            pieces = range(j * (TILE // DH), (j + 1) * (TILE // DH))
+            logs = jnp.concatenate([rows_in[level, i : i + 1, 0:DH] for i in pieces], axis=1)
+            deltas = jnp.concatenate([rows_in[level, i : i + 1, DH:] for i in pieces], axis=1)
+            q = q_in[level, qs, :]
+            do = do_in[level, :, qs]
+            s = dot(ka, jnp.concatenate([q, mq_far[level, qs, :]], axis=1), 1, 1)
+            probs = jnp.exp2((s - logs) * coef)
+            ds = (probs * (dot(v, do, 1, 0) - deltas)).astype(BF16)
+            dk_sum = dk_sum + dot(ds, q, 1, 0)
+            dv_sum = dv_sum + dot(probs.astype(BF16), do, 1, 1)
+        keep_grads(level, 1, dk_sum, dv_sum)
+
+    own_copies = [
+        pltpu.make_async_copy(gr_out.at[level, 1], gr_hbm.at[level, 1], io.at[3 + level])
+        for level in range(2)
+    ]
+    for copy in own_copies:
+        copy.start()
 
     for h in range(HEADS_DEV):
         gr_copy(2, h).wait()
@@ -460,8 +595,9 @@
     part_copy = pltpu.make_async_copy(dkv, part_hbm, io.at[2])
     part_copy.start()
     for level in range(2):
-        for h in range(HEADS_DEV):
-            gr_copy(level, h).wait()
+        gr_copy(level, 0).wait()
+    for copy in own_copies:
+        copy.wait()
     lo_copy.wait()
     dq_copy.wait()
     part_copy.wait()
@@ -551,16 +687,28 @@
         pltpu.VMEM((HEADS_DEV, 1, TOK), F32),
         pltpu.VMEM((COLS, TOK), F32),
         pltpu.VMEM((TOK, 2 * COLS), F32),
-        pltpu.VMEM((9, 8, COLS), F32),
+        pltpu.VMEM((8, 8, COLS), F32),
         pltpu.SMEM((TOK // BLOCK,), jnp.int32),
+        pltpu.VMEM((2, TOK, DH), BF16),
+        pltpu.VMEM((2, KEPT, DH), BF16),
+        pltpu.VMEM((2, TOK, DH), BF16),
+        pltpu.VMEM((2, DH, TOK), BF16),
+        pltpu.VMEM((8, 2 * DH), F32),
+        pltpu.VMEM((2, 8, 2 * DH), F32),
+        dma((2, HALVES)),
+        dma((2, HALVES)),
+        dma((2, HALVES)),
+        dma((2, HALVES)),
+        dma((2,)),
+        dma((2,)),
         dma((LEVELS, NCH)),
         dma((LEVELS, NCH)),
         dma((LEVELS, HEADS_DEV)),
         dma((LEVELS, HEADS_DEV)),
         dma((2, N_HEAD)),
         dma((2, N_HEAD)),
-        dma((4,)),
-        dma((4,)),
+        dma((5,)),
+        dma((5,)),
         dma((18,)),
     ]
     kept = jnp.transpose(kept_blocks, (1, 2, 0))

time: 67.6 us -> 65.5 us (0.969)
  Pallas kernels: 66.8 us -> 64.4 us
    pallas_call x1, Pallas kernels: 63.9 us -> 61.6 us  [local(): pl.pallas_call(kernel, out_shape=[pltpu.VMEM((TOK, COLS), BF16), pltpu.VM...]
where the time goes in v4:
time: 65.5 us; the launch traced here: 65.1 us
  Pallas kernels  64.4 us (98%)
    pallas_call x1, Pallas kernels, local(): pl.pallas_call(kernel, out_shape=[pltpu.VMEM((TOK, COLS), BF16), pltpu.VM...  61.6 us
    pallas_call x1, Pallas kernels, local(): pl.pallas_call(finish, out_shape=[rows, rows, rows, rows, gain_row], in_s...  2.86 us

profile of v4, /device:TPU:0, one launch (start us, length us, event | category | flops | bytes accessed | tf_op | source)
XLA Modules:
  0.0 65.1 jit_solution(2268448063925386079)
XLA Ops:
  0.6 61.6 %attention.1 = (bf16[1024,256]{1,0:T(8,128)(2,1)S(1)}, bf16[1024,256]{1,0:T(8,128)(2,1)S(1)}, f32[1024,512]{1,0:T(8,128)S(1)}, bf16[2,2,8,64,256]{4,3,2,1,0:T(8,128)(2,1)S(1)}, f32[1,256]{1,0:T(1,128)S(1)}) custom-call(s32[3,8,16]{2,1,0:T(8,128)} %bitcast.7, s32[3]{0:T(128)} %lengths.1, bf16[1024,256]{1,0:T(8,128)(2,1)} %q_hbm.1, ...), custom_call_target="tpu_custom_call" | custom-call | tf_op jit(solution)/shard_map/attention/pallas_call | solution.py:716
  62.2 2.9 %finish.1 = (bf16[1024,256]{1,0:T(8,128)(2,1)}, bf16[1024,256]{1,0:T(8,128)(2,1)}, bf16[1024,256]{1,0:T(8,128)(2,1)}, bf16[1024,256]{1,0:T(8,128)(2,1)}, f32[1,256]{1,0:T(1,128)}) custom-call(s32[3,8,16]{2,1,0:T(8,128)} %bitcast.8, bf16[1024,256]{1,0:T(8,128)(2,1)S(1)} %get-tuple-element.15.lo_in, bf16[1024,256]{1,0:T(8,128)(2,1)S(1)} %get-tuple-element.16.dq_in, ...), custom_call_target="tpu_custom_call" | custom-call | tf_op jit(solution)/shard_map/finish/pallas_call | solution.py:746

commit v5 on v4

--- a/solution.py
+++ b/solution.py
@@ -475,34 +475,28 @@
         gr_out[level, h, :, :, 0:DH] = (dk_sum * SCALE).astype(BF16).reshape(shape)
         gr_out[level, h, :, :, DH:] = dv_sum.astype(BF16).reshape(shape)
 
-    @pl.loop(0, 2)
-    def _(t):
-        level = 1 - t
-        back_level(level, 0, True)
-        for one in range(2):
-
-            @pl.when(level == one)
-            def _():
-                if one == 1:
-                    for c in range(HALVES):
-                        q_copy(0, c).wait()
-                        q_copy(1, c).start()
-                else:
-                    for stage in range(3):
-                        gg_copy(stage).wait()
-                    gsum[4] = (gsum[0] + gsum[1]) + (gsum[2] + gsum[3])
-                    gg_copy(3).start()
-                gr_copy(one, 0).start()
-
-    for h in range(HEADS_DEV):
-        back_level(2, h, True)
-        do_copy(0, h).wait()
-        do_copy(1, h).start()
-        if h == 0:
-            gg_copy(3).wait()
-            gsum[6] = gsum[4] + gsum[5]
-            gg_copy(4).start()
-        gr_copy(2, h).start()
+    back_level(0, 0, True)
+    for c in range(HALVES):
+        q_copy(0, c).wait()
+        q_copy(1, c).start()
+    gr_copy(0, 0).start()
+    back_level(2, 0, True)
+    for stage in range(3):
+        gg_copy(stage).wait()
+    gsum[4] = (gsum[0] + gsum[1]) + (gsum[2] + gsum[3])
+    gg_copy(3).start()
+    gr_copy(2, 0).start()
+    back_level(1, 0, True)
+    do_copy(0, 0).wait()
+    do_copy(1, 0).start()
+    gr_copy(1, 0).start()
+    back_level(2, 1, True)
+    do_copy(0, 1).wait()
+    do_copy(1, 1).start()
+    gg_copy(3).wait()
+    gsum[6] = gsum[4] + gsum[5]
+    gg_copy(4).start()
+    gr_copy(2, 1).start()
 
     @pl.loop(0, 2)
     def _(level):
@@ -541,6 +535,25 @@
     dq_copy.start()
     gg_copy(4).wait()
     gg_ref[...] = gsum[6, 0:1, :] + gsum[7, 0:1, :]
+
+    for h in range(HEADS_DEV):
+        gr_copy(2, h).wait()
+
+    @pl.loop(0, TOK // BLOCK)
+    def _(b):
+        slot = inv_slot[b]
+        rows = pl.ds(pl.multiple_of(b * BLOCK, BLOCK), BLOCK)
+        used = jnp.minimum(slot + 1, 1).astype(F32)
+        for h in range(HEADS_DEV):
+            part = gr_in2[h, jnp.maximum(slot, 0)].astype(F32) * used
+            dkv[rows, h * DH : (h + 1) * DH] += part[:, 0:DH]
+            dkv[rows, COLS + h * DH : COLS + (h + 1) * DH] += part[:, DH:]
+
+    part_copy = pltpu.make_async_copy(dkv, part_hbm, io.at[2])
+    part_copy.start()
+
+    def own_copy(level):
+        return pltpu.make_async_copy(gr_out.at[level, 1], gr_hbm.at[level, 1], io.at[3 + level])
 
     @pl.loop(0, 2)
     def _(level):
@@ -571,44 +584,41 @@
             dk_sum = dk_sum + dot(ds, q, 1, 0)
             dv_sum = dv_sum + dot(probs.astype(BF16), do, 1, 1)
         keep_grads(level, 1, dk_sum, dv_sum)
-
-    own_copies = [
-        pltpu.make_async_copy(gr_out.at[level, 1], gr_hbm.at[level, 1], io.at[3 + level])
-        for level in range(2)
-    ]
-    for copy in own_copies:
-        copy.start()
-
-    for h in range(HEADS_DEV):
-        gr_copy(2, h).wait()
-
-    @pl.loop(0, TOK // BLOCK)
-    def _(b):
-        slot = inv_slot[b]
-        rows = pl.ds(pl.multiple_of(b * BLOCK, BLOCK), BLOCK)
-        used = jnp.minimum(slot + 1, 1).astype(F32)
-        for h in range(HEADS_DEV):
-            part = gr_in2[h, jnp.maximum(slot, 0)].astype(F32) * used
-            dkv[rows, h * DH : (h + 1) * DH] += part[:, 0:DH]
-            dkv[rows, COLS + h * DH : COLS + (h + 1) * DH] += part[:, DH:]
-
-    part_copy = pltpu.make_async_copy(dkv, part_hbm, io.at[2])
-    part_copy.start()
+        for one in range(2):
+            pl.when(level == one)(lambda one=one: own_copy(one).start())
+
     for level in range(2):
         gr_copy(level, 0).wait()
-    for copy in own_copies:
-        copy.wait()
+    for level in range(2):
+        own_copy(level).wait()
     lo_copy.wait()
     dq_copy.wait()
     part_copy.wait()
 
 
 def finish(
-    kept, lo_in, dq_in, part_in, gr_in, gg_in, lo_ref, dq_ref, dk_ref, dv_ref, gg_ref, dk, dv, sems
+    kept_hbm,
+    lo_in,
+    dq_in,
+    part_in,
+    gr_in,
+    gg_in,
+    lo_ref,
+    dq_ref,
+    dk_ref,
+    dv_ref,
+    gg_ref,
+    kept,
+    dk,
+    dv,
+    sems,
+    few,
 ):
     me = lax.axis_index("seq")
-    gg_ref[...] = gg_in[...]
-    copies = []
+    kept_copy = pltpu.make_async_copy(kept_hbm, kept, few.at[0])
+    kept_copy.start()
+    copies = [pltpu.make_async_copy(gg_in, gg_ref, few.at[1])]
+    copies[0].start()
 
     def send(src, dst, i, lane):
         rows = pl.ds(i * TILE, TILE)
@@ -619,6 +629,7 @@
     for i in range(TOK // TILE):
         send(lo_in, lo_ref, i, 0)
         send(dq_in, dq_ref, i, 1)
+    kept_copy.wait()
     for i in range(TOK // TILE):
         for b in range(i * (TILE // BLOCK), (i + 1) * (TILE // BLOCK)):
             rows = slice(b * BLOCK, (b + 1) * BLOCK)
@@ -746,12 +757,14 @@
     lo, dq, dk, dv, gain = pl.pallas_call(
         finish,
         out_shape=[rows, rows, rows, rows, gain_row],
-        in_specs=[smem] + [vmem] * 5,
-        out_specs=[hbm] * 4 + [vmem],
+        in_specs=[hbm] + [vmem] * 5,
+        out_specs=[hbm] * 5,
         scratch_shapes=[
+            pltpu.SMEM((LEVELS, KEEP, N_SEQ), jnp.int32),
             pltpu.VMEM((TOK, COLS), BF16),
             pltpu.VMEM((TOK, COLS), BF16),
             dma((4, TOK // TILE)),
+            dma((2,)),
         ],
         compiler_params=pltpu.CompilerParams(vmem_limit_bytes=12 * 1024 * 1024),
         name="finish",

time: 65.5 us -> 63.9 us (0.976)
  Pallas kernels: 64.4 us -> 63.1 us
    pallas_call x1, Pallas kernels: 61.6 us -> 60.9 us  [local(): pl.pallas_call(kernel, out_shape=[pltpu.VMEM((TOK, COLS), BF16), pltpu.VM...]
    pallas_call x1, Pallas kernels: 2.86 us -> 2.19 us  [local(): pl.pallas_call(finish, out_shape=[rows, rows, rows, rows, gain_row], in_s...]
where the time goes in v5:
time: 63.9 us; the launch traced here: 63.7 us
  Pallas kernels  63.1 us (99%)
  between operations  0.64 us (1%)
    pallas_call x1, Pallas kernels, local(): pl.pallas_call(kernel, out_shape=[pltpu.VMEM((TOK, COLS), BF16), pltpu.VM...  60.9 us
    pallas_call x1, Pallas kernels, local(): pl.pallas_call(finish, out_shape=[rows, rows, rows, rows, gain_row], in_s...  2.19 us

profile of v5, /device:TPU:0, one launch (start us, length us, event | category | flops | bytes accessed | tf_op | source)
XLA Modules:
  0.0 63.7 jit_solution(8476026677334515918)
XLA Ops:
  0.6 60.9 %attention.1 = (bf16[1024,256]{1,0:T(8,128)(2,1)S(1)}, bf16[1024,256]{1,0:T(8,128)(2,1)S(1)}, f32[1024,512]{1,0:T(8,128)S(1)}, bf16[2,2,8,64,256]{4,3,2,1,0:T(8,128)(2,1)S(1)}, f32[1,256]{1,0:T(1,128)S(1)}) custom-call(s32[3,8,16]{2,1,0:T(8,128)} %bitcast.7, s32[3]{0:T(128)} %lengths.1, bf16[1024,256]{1,0:T(8,128)(2,1)} %q_hbm.1, ...), custom_call_target="tpu_custom_call" | custom-call | tf_op jit(solution)/shard_map/attention/pallas_call | solution.py:727
  61.5 2.2 %finish.1 = (bf16[1024,256]{1,0:T(8,128)(2,1)}, bf16[1024,256]{1,0:T(8,128)(2,1)}, bf16[1024,256]{1,0:T(8,128)(2,1)}, bf16[1024,256]{1,0:T(8,128)(2,1)}, f32[1,256]{1,0:T(1,128)}) custom-call(s32[3,8,16]{2,1,0:T(8,128)} %bitcast.8, bf16[1024,256]{1,0:T(8,128)(2,1)S(1)} %get-tuple-element.15.lo_in, bf16[1024,256]{1,0:T(8,128)(2,1)S(1)} %get-tuple-element.16.dq_in, ...), custom_call_target="tpu_custom_call" | custom-call | tf_op jit(solution)/shard_map/finish/pallas_call | solution.py:757

commit v6 on v5

--- a/solution.py
+++ b/solution.py
@@ -51,7 +51,7 @@
 
 def kernel(
     kept_hbm,
-    lengths,
+    lengths_hbm,
     q_hbm,
     k_hbm,
     v_hbm,
@@ -63,6 +63,7 @@
     gr_hbm,
     gg_ref,
     kept,
+    lengths,
     q_ref,
     k_ref,
     v_ref,
@@ -145,15 +146,10 @@
 
     loads = load(k_hbm, k_ref, 4, 0) + load(v_hbm, v_ref, 4, 4) + load(kept_hbm, kept, 1, 8)
     later = load(q_hbm, q_ref, 4, 9) + load(g_hbm, g_ref, 4, 13) + load(gain_hbm, gain_ref, 1, 17)
+    lengths_copy = pltpu.make_async_copy(lengths_hbm, lengths, io.at[18])
+    lengths_copy.start()
     for copy in loads:
         copy.wait()
-
-    for level in range(LEVELS):
-        for slot in range(KEEP):
-            block = jnp.maximum(kept[level, slot, me], 0)
-            kv_out[level, slot * BLOCK : (slot + 1) * BLOCK, 0:COLS] = k_ref[block]
-            kv_out[level, slot * BLOCK : (slot + 1) * BLOCK, COLS:] = v_ref[block]
-    pl.semaphore_wait(barrier, 5 + N_HEAD - 1)
 
     def kv_copy(level, c):
         rows = pl.ds(pl.multiple_of(c * CHUNK, CHUNK), CHUNK)
@@ -211,8 +207,15 @@
 
     for c in range(NCH):
         for level in (1, 0, 2):
+            for slot in range(c * KEEP // NCH, (c + 1) * KEEP // NCH):
+                block = jnp.maximum(kept[level, slot, me], 0)
+                kv_out[level, slot * BLOCK : (slot + 1) * BLOCK, 0:COLS] = k_ref[block]
+                kv_out[level, slot * BLOCK : (slot + 1) * BLOCK, COLS:] = v_ref[block]
+            if c == 0 and level == 1:
+                pl.semaphore_wait(barrier, 5 + N_HEAD - 1)
             kv_copy(level, c).start()
 
+    lengths_copy.wait()
     for copy in later:
         copy.wait()
     start1 = lengths[0]
@@ -656,13 +659,13 @@
 
 def local(query_rows, key_rows, value_rows, norm_gain, grad_out, doc_lengths, kept_blocks):
     vmem = pl.BlockSpec(memory_space=pltpu.VMEM)
-    smem = pl.BlockSpec(memory_space=pltpu.SMEM)
     hbm = pl.BlockSpec(memory_space=pltpu.HBM)
     some = pl.BlockSpec(memory_space=pl.ANY)
     rows = jax.ShapeDtypeStruct((TOK, COLS), BF16)
     dma = pltpu.SemaphoreType.DMA
     scratch = [
         pltpu.SMEM((LEVELS, KEEP, N_SEQ), jnp.int32),
+        pltpu.SMEM((3,), jnp.int32),
         pltpu.VMEM((TOK, COLS), BF16),
         pltpu.VMEM((TOK // BLOCK, BLOCK, COLS), BF16),
         pltpu.VMEM((TOK // BLOCK, BLOCK, COLS), BF16),
@@ -720,7 +723,7 @@
         dma((2, N_HEAD)),
         dma((5,)),
         dma((5,)),
-        dma((18,)),
+        dma((19,)),
     ]
     kept = jnp.transpose(kept_blocks, (1, 2, 0))
     gain_row = jax.ShapeDtypeStruct((1, COLS), F32)
@@ -733,7 +736,7 @@
             pltpu.VMEM((2, HEADS_DEV, KEEP, BLOCK, 2 * DH), BF16),
             pltpu.VMEM((1, COLS), F32),
         ],
-        in_specs=[hbm, smem] + [hbm] * 5,
+        in_specs=[hbm] * 7,
         out_specs=[some] * 4 + [vmem],
         scratch_shapes=scratch,
         compiler_params=pltpu.CompilerParams(

time: 63.9 us -> 63.3 us (level)
  Pallas kernels: 63.1 us -> 62.4 us
    pallas_call x1, Pallas kernels: 60.9 us -> 60.2 us  [local(): pl.pallas_call(kernel, out_shape=[pltpu.VMEM((TOK, COLS), BF16), pltpu.VM...]
where the time goes in v6:
time: 63.3 us; the launch traced here: 63.1 us
  Pallas kernels  62.4 us (99%)
  between operations  0.64 us (1%)
    pallas_call x1, Pallas kernels, local(): pl.pallas_call(kernel, out_shape=[pltpu.VMEM((TOK, COLS), BF16), pltpu.VM...  60.2 us
    pallas_call x1, Pallas kernels, local(): pl.pallas_call(finish, out_shape=[rows, rows, rows, rows, gain_row], in_s...  2.19 us

profile of v6, /device:TPU:0, one launch (start us, length us, event | category | flops | bytes accessed | tf_op | source)
XLA Modules:
  0.0 63.1 jit_solution(14375666339534668711)
XLA Ops:
  0.6 60.2 %attention.1 = (bf16[1024,256]{1,0:T(8,128)(2,1)S(1)}, bf16[1024,256]{1,0:T(8,128)(2,1)S(1)}, f32[1024,512]{1,0:T(8,128)S(1)}, bf16[2,2,8,64,256]{4,3,2,1,0:T(8,128)(2,1)S(1)}, f32[1,256]{1,0:T(1,128)S(1)}) custom-call(s32[3,8,16]{2,1,0:T(8,128)} %bitcast.7, s32[3]{0:T(128)} %lengths_hbm.1, bf16[1024,256]{1,0:T(8,128)(2,1)} %q_hbm.1, ...), custom_call_target="tpu_custom_call" | custom-call | tf_op jit(solution)/shard_map/attention/pallas_call | solution.py:730
  60.9 2.2 %finish.1 = (bf16[1024,256]{1,0:T(8,128)(2,1)}, bf16[1024,256]{1,0:T(8,128)(2,1)}, bf16[1024,256]{1,0:T(8,128)(2,1)}, bf16[1024,256]{1,0:T(8,128)(2,1)}, f32[1,256]{1,0:T(1,128)}) custom-call(s32[3,8,16]{2,1,0:T(8,128)} %bitcast.8, bf16[1024,256]{1,0:T(8,128)(2,1)S(1)} %get-tuple-element.15.lo_in, bf16[1024,256]{1,0:T(8,128)(2,1)S(1)} %get-tuple-element.16.dq_in, ...), custom_call_target="tpu_custom_call" | custom-call | tf_op jit(solution)/shard_map/finish/pallas_call | solution.py:760

commit v7 on v6

--- a/solution.py
+++ b/solution.py
@@ -623,8 +623,8 @@
     copies = [pltpu.make_async_copy(gg_in, gg_ref, few.at[1])]
     copies[0].start()
 
-    def send(src, dst, i, lane):
-        rows = pl.ds(i * TILE, TILE)
+    def send(src, dst, i, lane, size=TILE):
+        rows = pl.ds(i * size, size)
         copy = pltpu.make_async_copy(src.at[rows], dst.at[rows], sems.at[lane, i])
         copy.start()
         copies.append(copy)
@@ -633,8 +633,8 @@
         send(lo_in, lo_ref, i, 0)
         send(dq_in, dq_ref, i, 1)
     kept_copy.wait()
-    for i in range(TOK // TILE):
-        for b in range(i * (TILE // BLOCK), (i + 1) * (TILE // BLOCK)):
+    for i in range(TOK // DH):
+        for b in range(i * (DH // BLOCK), (i + 1) * (DH // BLOCK)):
             rows = slice(b * BLOCK, (b + 1) * BLOCK)
             total = part_in[rows, :]
             key = [total[:, h * DH : (h + 1) * DH] for h in range(HEADS_DEV)]
@@ -651,8 +651,8 @@
             for h in range(HEADS_DEV):
                 dk[rows, h * DH : (h + 1) * DH] = key[h].astype(BF16)
                 dv[rows, h * DH : (h + 1) * DH] = value[h].astype(BF16)
-        send(dk, dk_ref, i, 2)
-        send(dv, dv_ref, i, 3)
+        send(dk, dk_ref, i, 2, DH)
+        send(dv, dv_ref, i, 3, DH)
     for copy in copies:
         copy.wait()
 
@@ -766,7 +766,7 @@
             pltpu.SMEM((LEVELS, KEEP, N_SEQ), jnp.int32),
             pltpu.VMEM((TOK, COLS), BF16),
             pltpu.VMEM((TOK, COLS), BF16),
-            dma((4, TOK // TILE)),
+            dma((4, TOK // DH)),
             dma((2,)),
         ],
         compiler_params=pltpu.CompilerParams(vmem_limit_bytes=12 * 1024 * 1024),

time: 63.3 us -> 63.4 us (level)
  no operation moved by 1% of the time
where the time goes in v7:
time: 63.4 us; the launch traced here: 63.2 us
  Pallas kernels  62.5 us (99%)
  between operations  0.64 us (1%)
    pallas_call x1, Pallas kernels, local(): pl.pallas_call(kernel, out_shape=[pltpu.VMEM((TOK, COLS), BF16), pltpu.VM...  60.2 us
    pallas_call x1, Pallas kernels, local(): pl.pallas_call(finish, out_shape=[rows, rows, rows, rows, gain_row], in_s...  2.31 us

profile of v7, /device:TPU:0, one launch (start us, length us, event | category | flops | bytes accessed | tf_op | source)
XLA Modules:
  0.0 63.2 jit_solution(7460155986270867009)
XLA Ops:
  0.6 60.2 %attention.1 = (bf16[1024,256]{1,0:T(8,128)(2,1)S(1)}, bf16[1024,256]{1,0:T(8,128)(2,1)S(1)}, f32[1024,512]{1,0:T(8,128)S(1)}, bf16[2,2,8,64,256]{4,3,2,1,0:T(8,128)(2,1)S(1)}, f32[1,256]{1,0:T(1,128)S(1)}) custom-call(s32[3,8,16]{2,1,0:T(8,128)} %bitcast.7, s32[3]{0:T(128)} %lengths_hbm.1, bf16[1024,256]{1,0:T(8,128)(2,1)} %q_hbm.1, ...), custom_call_target="tpu_custom_call" | custom-call | tf_op jit(solution)/shard_map/attention/pallas_call | solution.py:730
  60.9 2.3 %finish.1 = (bf16[1024,256]{1,0:T(8,128)(2,1)}, bf16[1024,256]{1,0:T(8,128)(2,1)}, bf16[1024,256]{1,0:T(8,128)(2,1)}, bf16[1024,256]{1,0:T(8,128)(2,1)}, f32[1,256]{1,0:T(1,128)}) custom-call(s32[3,8,16]{2,1,0:T(8,128)} %bitcast.8, bf16[1024,256]{1,0:T(8,128)(2,1)S(1)} %get-tuple-element.15.lo_in, bf16[1024,256]{1,0:T(8,128)(2,1)S(1)} %get-tuple-element.16.dq_in, ...), custom_call_target="tpu_custom_call" | custom-call | tf_op jit(solution)/shard_map/finish/pallas_call | solution.py:760
